TPU v7x, 128 devices: a whole 4x4x4 slice. The times are simulated.
128 devices in a mesh: ind: 64 (over y, x, z), snp: 2 (over core).
Axes of the slice: x: 4, y: 4, z: 4, core: 2. Of those that a mesh axis runs over, the one named last changes fastest.
Arguments:
- genotypes: bfloat16 [2, 249856, 1024], P(None, 'ind', 'snp'), may hold values from -0.013387887 to 0.013387887
- residual: float32 [32, 249856], P(None, 'ind'), may hold values from -7 to 7
- effects: float32 [2, 32, 1024], P(None, None, 'snp'), may hold values from -6 to 6
- noise: float32 [2, 32, 1024], replicated, may hold values from -6 to 6
- prior_var: float32 [2048], replicated, may hold values from 0.1 to 2
- block_snps: int32 [2048], replicated, may hold values from 0 to 2047, each once
- noise_var: float32 [32], replicated, may hold values from 0.5 to 2
- chi_scaled: float32 [32], replicated, may hold values from 0.8 to 1.25
Outputs:
- new_effects: float32 [2, 32, 1024], P(None, None, 'snp')
- new_residual: float32 [32, 249856], P(None, 'ind')
- variance_draw: float32 [32], replicated
Inputs may be any that keep to these rules, and one draw needn't show every extreme that they name: `block_snps`: every table row appears once; entries b * 1024 to (b + 1) * 1024 - 1 belong to block b.
All inputs are finite; a program needn't handle non-finite values.
Results may differ from a plain program's by a relative error of at most 0.004.
Values may be sent and summed in bfloat16 or wider, within the bound.
No kernel may reach another device: no remote copies, remote signals or barrier semaphores. Data moves between devices by JAX's collectives and lax.ppermute only.
A program may use at most 192 MiB of HBM per device.

v0:
```python
import functools

import jax
import jax.numpy as jnp
from jax import lax
from jax.experimental import pallas as pl
from jax.experimental.pallas import tpu as pltpu
from jax.sharding import PartitionSpec as P

F32 = jnp.float32
BF16 = jnp.bfloat16
TILE = 128
SUB = 8
STRIP = 256
CHUNK = 1024
LINE = 4
NT = (((1,), (1,)), ((), ()))
NN = (((1,), (0,)), ((), ()))
TN = (((0,), (0,)), ((), ()))
VMEM = pl.BlockSpec(memory_space=pltpu.VMEM)
SMEM = pl.BlockSpec(memory_space=pltpu.SMEM)
ANY = pl.BlockSpec(memory_space=pl.ANY)
PARAMS = pltpu.CompilerParams(vmem_limit_bytes=52 * 2**20)


def dot_exact(left, right, dims):
    return lax.dot_general(
        left, right, dims, preferred_element_type=F32, precision=lax.Precision.HIGHEST
    )


def dot_bf16(left, right, dims):
    return lax.dot_general(left, right, dims, preferred_element_type=F32)


def spread(row):
    return jnp.broadcast_to(row, (SUB, TILE))


def pieces_of(value):
    high = value.astype(BF16)
    rest = value - high.astype(F32)
    middle = rest.astype(BF16)
    return high, middle, (rest - middle.astype(F32)).astype(BF16)


def dot_rows(left, right, dims):
    rows = left.shape[0]
    parts = pieces_of(left)
    high, middle, low = pieces_of(right)
    one = dot_bf16(jnp.concatenate(parts, axis=0), high, dims)
    two = dot_bf16(jnp.concatenate(parts[:2], axis=0), middle, dims)
    three = dot_bf16(parts[0], low, dims)
    return one[:rows] + ((one[rows : 2 * rows] + two[:rows]) + (one[2 * rows :] + two[rows:] + three))


def tree_sum(terms):
    while len(terms) > 1:
        terms = [terms[i] + terms[i + 1] if i + 1 < len(terms) else terms[i] for i in range(0, len(terms), 2)]
    return terms[0]


def inverse_factor(tile, zero):
    groups = TILE // SUB
    sub = lax.broadcasted_iota(jnp.int32, (SUB, TILE), 0)
    lane = lax.broadcasted_iota(jnp.int32, (SUB, TILE), 1)
    left = [tile[SUB * r : SUB * r + SUB, :] for r in range(groups)]
    done = []
    for g in range(groups):
        first = g * SUB
        inside = (lane >= first) & (lane < first + SUB)
        pivot_cols = [spread(left[g][:, first + j : first + j + 1]) + zero for j in range(SUB)]
        cols = [[spread(left[r][:, first + j : first + j + 1]) for r in range(g + 1, groups)] for j in range(SUB)]
        square = {(i, j): spread(pivot_cols[j][i : i + 1, :]) for j in range(SUB) for i in range(j + 1)}
        own = jnp.where(inside, jnp.where(lane == sub + first, 1.0, 0.0), left[g])
        rows = [spread(own[j : j + 1, :]) for j in range(SUB)]
        last = g + 1 == groups
        near = None if last else [cols[j][0] for j in range(SUB)]
        near_terms = []
        share = {}
        solved = [None] * SUB
        pivots = jnp.zeros((SUB, TILE), F32)
        finished = pivots
        for j in range(0, SUB, 2):
            p, q, r = square[j, j], square[j, j + 1], square[j + 1, j + 1]
            minor = p * r - q * q
            over_minor = pltpu.reciprocal(minor, approx=True)
            over_p = pltpu.reciprocal(p, approx=True)
            ip, iq, ir = r * over_minor, -q * over_minor, p * over_minor
            pivots = jnp.where(sub == j, p, jnp.where(sub == j + 1, minor * over_p, pivots))
            second_row = rows[j + 1] - (q * over_p) * rows[j]
            finished = jnp.where(sub == j, rows[j], jnp.where(sub == j + 1, second_row, finished))
            for k in range(j + 2, SUB):
                upper, lower = square[j, k], square[j + 1, k]
                share[j, k], share[j + 1, k] = upper * ip + lower * iq, upper * iq + lower * ir
            for k in range(j + 2, SUB):
                one, two = share[j, k], share[j + 1, k]
                for i in range(j + 2, k + 1):
                    square[i, k] = square[i, k] - (square[j, i] * one + square[j + 1, i] * two)
                rows[k] = rows[k] - (rows[j] * one + rows[j + 1] * two)
                if not last:
                    near[k] = near[k] - (near[j] * one + near[j + 1] * two)
            solved[j], solved[j + 1] = rows[j] * ip + rows[j + 1] * iq, rows[j] * iq + rows[j + 1] * ir
            if not last:
                near_terms.append(near[j] * solved[j] + near[j + 1] * solved[j + 1])
        if not last:
            left[g + 1] = jnp.where(inside, 0.0, left[g + 1]) - tree_sum(near_terms)
        for j in (4, 5, 2, 3, 0, 1):
            solved[j] = solved[j] - tree_sum([share[j, k] * solved[k] for k in range(j // 2 * 2 + 2, SUB)])
        for r in range(g + 2, groups):
            left[r] = jnp.where(inside, 0.0, left[r]) - tree_sum([cols[j][r - g - 1] * solved[j] for j in range(SUB)])
        root = lax.rsqrt(pivots)
        root = root * (1.5 - 0.5 * pivots * root * root)
        done.append(jnp.where(lane < first + SUB, finished * root, 0.0))
    return jnp.concatenate(done, axis=0)


def split_scores(residual, x):
    high, middle, _ = pieces_of(residual)
    return dot_bf16(high, x, NN) + dot_bf16(middle, x, NN)


def chunk_loop(rows, body):
    whole = rows // CHUNK

    @pl.loop(0, whole)
    def _(i):
        body(i, pl.multiple_of(i * CHUNK, CHUNK), CHUNK)

    if rows % CHUNK:
        body(whole, whole * CHUNK, rows % CHUNK)


def start_copies(sources, places, sems, rows):
    copies = []
    for i, lo in enumerate(range(0, rows, CHUNK)):
        at = pl.ds(lo, min(CHUNK, rows - lo))
        for k, (source, place) in enumerate(zip(sources, places)):
            pltpu.make_async_copy(source.at[at, :], place.at[at, :], sems.at[i, k]).start()


def wait_copies(sources, places, sems, i, start, size):
    at = pl.ds(start, size)
    for k, (source, place) in enumerate(zip(sources, places)):
        pltpu.make_async_copy(source.at[at, :], place.at[at, :], sems.at[i, k]).wait()


def own_kernel(core_ref, own_ref, residual_ref, square_ref, score_ref, cross_ref, mine, sems):
    core = core_ref[0]
    rows, half = own_ref.shape[1:]
    sources, places = [own_ref.at[0], own_ref.at[1]], [mine.at[0], mine.at[1]]
    start_copies(sources, places, sems, rows)
    for ref in (square_ref, score_ref, cross_ref):
        ref[...] = jnp.zeros_like(ref)

    def body(i, start, size):
        wait_copies(sources, places, sems, i, start, size)
        at = pl.ds(start, size)
        score_ref[...] += split_scores(residual_ref[:, at], mine[core, at, :])
        cross_ref[...] += dot_bf16(mine[0, at, :], mine[1, at, :], TN)
        for c in range(0, half, STRIP):
            square_ref[c:, c : c + STRIP] += dot_bf16(mine[core, at, c:], mine[core, at, c : c + STRIP], TN)

    chunk_loop(rows, body)


class Layout:
    def __init__(self, count, chains, spots):
        self.count, self.chains = count, chains
        self.pairs = count * (count - 1) // 2 * TILE
        self.diagonals = self.pairs + count // 2 * TILE
        self.scores = self.diagonals + SUB
        self.squares = self.scores + count * chains
        self.used = self.squares + chains
        self.piece = -(-self.used // (spots * SUB)) * SUB
        self.rows = self.piece * spots

    def lower(self, row, col):
        return (row * (row - 1) // 2 + col) * TILE


def put_diagonal(packed_ref, layout, half_at, block):
    count = layout.count // 2
    row_id = lax.broadcasted_iota(jnp.int32, (TILE, TILE), 0)
    col_id = lax.broadcasted_iota(jnp.int32, (TILE, TILE), 1)
    for r in range(count):
        for c in range(r):
            row, col = half_at * count + r, half_at * count + c
            at = pl.multiple_of((lax.shift_right_logical(row * (row - 1), 1) + col) * TILE, TILE)
            packed_ref[pl.ds(at, TILE), :] = block[r * TILE : r * TILE + TILE, c * TILE : c * TILE + TILE]
    for r in range(0, count, 2):
        one = block[r * TILE : r * TILE + TILE, r * TILE : r * TILE + TILE]
        two = block[(r + 1) * TILE : (r + 2) * TILE, (r + 1) * TILE : (r + 2) * TILE]
        place = half_at * (count // 2) + r // 2
        at = pl.multiple_of(layout.pairs + place * TILE, TILE)
        packed_ref[pl.ds(at, TILE), :] = jnp.where(row_id > col_id, one, two)
        packed_ref[pl.ds(layout.diagonals + place, 1), :] = jnp.sum(
            jnp.where(row_id == col_id, one, 0.0), axis=0, keepdims=True
        )


def get_diagonal(packed_ref, layout, tile):
    row_id = lax.broadcasted_iota(jnp.int32, (TILE, TILE), 0)
    col_id = lax.broadcasted_iota(jnp.int32, (TILE, TILE), 1)
    at = layout.pairs + tile // 2 * TILE
    pair = packed_ref[at : at + TILE, :]
    if tile % 2:
        return jnp.where(row_id < col_id, pair, 0.0), jnp.where(row_id == col_id, pair, 0.0)
    row = layout.diagonals + tile // 2
    return jnp.where(row_id > col_id, pair, 0.0), jnp.where(row_id == col_id, packed_ref[row : row + 1, :], 0.0)


def gram_kernel(
    layout, core_ref, own_ref, other_ref, residual_ref, square_ref, own_score_ref, packed_ref, x, total, score, norm, sems
):
    core = core_ref[0]
    rows, half = own_ref.shape[1:]
    sources = [own_ref.at[core], other_ref.at[core]]
    places = [x.at[:, :half], x.at[:, half:]]
    start_copies(sources, places, sems, rows)
    for ref in (total, score, norm):
        ref[...] = jnp.zeros_like(ref)

    def body(i, start, size):
        wait_copies(sources, places, sems, i, start, size)
        at = pl.ds(start, size)
        total[...] += dot_bf16(x[at, half:], x[at, :], TN)
        score[...] += split_scores(residual_ref[:, at], x[at, half:])
        norm[...] += jnp.sum(jnp.square(residual_ref[:, at]), axis=1, keepdims=True)

    chunk_loop(rows, body)
    count, chains = layout.count, layout.chains
    put_diagonal(packed_ref, layout, core, square_ref)
    put_diagonal(packed_ref, layout, 1 - core, total.at[:, half:])
    for r in range(count // 2):
        for c in range(count // 2):
            at = layout.lower(count // 2 + r, c)

            @pl.when(core == 0)
            def _():
                packed_ref[at : at + TILE, :] = total[r * TILE : r * TILE + TILE, c * TILE : c * TILE + TILE]

            @pl.when(core == 1)
            def _():
                packed_ref[at : at + TILE, :] = total[c * TILE : c * TILE + TILE, r * TILE : r * TILE + TILE].T

    for k, part in ((core, own_score_ref), (1 - core, score)):
        for col in range(count // 2):
            start_row = pl.multiple_of(layout.scores + (k * (count // 2) + col) * chains, SUB)
            packed_ref[pl.ds(start_row, chains), :] = part[:, col * TILE : col * TILE + TILE]
    packed_ref[layout.squares : layout.used, :] = jnp.broadcast_to(norm[...], (chains, TILE))
    packed_ref[layout.used :, :] = jnp.zeros((layout.rows - layout.used, TILE), F32)


def cross_kernel(own_ref, other_ref, own_cross_ref, cross_ref, x, sems):
    rows = own_ref.shape[1]
    sources, places = [other_ref.at[0], own_ref.at[1]], [x.at[0], x.at[1]]
    start_copies(sources, places, sems, rows)
    cross_ref[0] = own_cross_ref[...]
    cross_ref[1] = jnp.zeros(own_cross_ref.shape, F32)

    def body(i, start, size):
        wait_copies(sources, places, sems, i, start, size)
        at = pl.ds(start, size)
        cross_ref[1] += dot_bf16(x[0, at, :], x[1, at, :], TN)

    chunk_loop(rows, body)


def backward(moved, factor_ref, inverse_ref, count):
    solved = [None] * count
    for k in reversed(range(count)):
        solved[k] = dot_rows(moved[k], inverse_ref[k], NN)
        if k:
            share = dot_rows(solved[k], factor_ref[k * TILE : k * TILE + TILE, : k * TILE], NN)
            for j in range(k):
                moved[j] = moved[j] - share[:, j * TILE : j * TILE + TILE]
    return solved


def factor_kernel(
    layout, packed_ref, prior_ref, rows_ref, effects_ref, noise_ref, scale_ref, factor_ref, inverse_ref, shift_ref, zero_ref
):
    width = factor_ref.shape[1]
    count = width // TILE
    chains = effects_ref.shape[0]
    table_rows = rows_ref[...]
    high = lax.shift_right_logical(table_rows, 7)
    low = lax.bitwise_and(table_rows, TILE - 1)
    prior = jnp.zeros((count, TILE), F32)
    for t in range(prior_ref.shape[0]):
        entry = jnp.broadcast_to(prior_ref[t : t + 1, :], (count, TILE))
        prior = jnp.where(high == t, jnp.take_along_axis(entry, low, axis=1), prior)
    inverse_prior = 1.0 / prior
    diagonal = lax.broadcasted_iota(jnp.int32, (TILE, TILE), 0) == lax.broadcasted_iota(jnp.int32, (TILE, TILE), 1)
    for row in range(count):
        rows = slice(row * TILE, row * TILE + TILE)
        for col in range(row):
            at = layout.lower(row, col)
            factor_ref[rows, col * TILE : col * TILE + TILE] = packed_ref[at : at + TILE, :]
        triangle, middle = get_diagonal(packed_ref, layout, row)
        middle = middle + jnp.where(diagonal, inverse_prior[row : row + 1, :], 0.0)
        factor_ref[rows, rows] = triangle + triangle.T + middle
        at = layout.scores + row * chains
        factor_ref[width : width + chains, rows] = (
            packed_ref[at : at + chains, :] - inverse_prior[row : row + 1, :] * effects_ref[:, rows]
        )
    zero_ref[...] = jnp.zeros_like(zero_ref)

    @pl.loop(0, count)
    def _(k):
        at = pl.multiple_of(k * TILE, TILE)
        inverse_ref[k] = inverse_factor(factor_ref[pl.ds(at, TILE), pl.ds(at, TILE)], zero_ref[...])
        for step in range(count):

            @pl.when(k == step)
            def _():
                lo = (step + 1) * TILE
                factor_ref[lo:, step * TILE : lo] = dot_exact(factor_ref[lo:, step * TILE : lo], inverse_ref[step], NT)
                if step % 2 == 0:
                    panel = factor_ref[lo:, step * TILE : lo]
                    factor_ref[lo:, lo : lo + TILE] = factor_ref[lo:, lo : lo + TILE] - dot_exact(panel, panel[:TILE, :], NT)
                else:
                    for c in range(lo, width, STRIP):
                        end = min(c + STRIP, width)
                        panel = factor_ref[c:, (step - 1) * TILE : lo]
                        factor_ref[c:, c:end] = factor_ref[c:, c:end] - dot_exact(panel, panel[: end - c, :], NT)

    scale = scale_ref[...]
    moved = [
        factor_ref[width : width + chains, j * TILE : j * TILE + TILE] + scale * noise_ref[:, j * TILE : j * TILE + TILE]
        for j in range(count)
    ]
    for j, part in enumerate(backward(moved, factor_ref, inverse_ref, count)):
        shift_ref[:, j * TILE : j * TILE + TILE] = part


def cross_share_kernel(core_ref, shift_ref, got_ref, cross_ref, share_ref):
    core = core_ref[0]
    half = cross_ref.shape[1]
    shift = jnp.where(core == 0, shift_ref[...], got_ref[...])
    change = shift.astype(BF16)
    first, last = change[:, :half], change[:, half:]
    mine = jnp.where(core == 0, first, last)
    theirs = jnp.where(core == 0, last, first)
    share_ref[...] = sum(
        dot_bf16(change, part, NN) for change, ref in ((mine, cross_ref[0]), (theirs, cross_ref[1])) for part in pieces_of(ref)
    )


def second_kernel(core_ref, shift_ref, share_ref, got_ref, factor_ref, inverse_ref, final_ref, share_all_ref):
    width = factor_ref.shape[1]
    count = width // TILE
    keep = jnp.where(core_ref[0] == 1, 1.0, 0.0)
    right = jnp.concatenate([got_ref[...], share_ref[...]], axis=1) * keep
    share_all_ref[...] = right
    moved = [right[:, j * TILE : j * TILE + TILE] for j in range(count)]
    for k in range(count):
        moved[k] = dot_rows(moved[k], inverse_ref[k], NT)
        lo = (k + 1) * TILE
        if lo < width:
            change_by = dot_rows(moved[k], factor_ref[lo:width, k * TILE : lo], NT)
            for j in range(k + 1, count):
                moved[j] = moved[j] - change_by[:, (j - k - 1) * TILE : (j - k) * TILE]
    for j, part in enumerate(backward(moved, factor_ref, inverse_ref, count)):
        cols = slice(j * TILE, j * TILE + TILE)
        final_ref[:, cols] = shift_ref[:, cols] - part


def squares_kernel(layout, final_ref, share_ref, packed_ref, squares_ref):
    count, chains = layout.count, layout.chains
    change = final_ref[...].astype(BF16)
    value = change.astype(F32)
    total = jnp.zeros((chains, TILE), F32)
    for row in range(count):
        cols = slice(row * TILE, row * TILE + TILE)
        triangle, middle = get_diagonal(packed_ref, layout, row)
        tiles = [packed_ref[layout.lower(row, col) : layout.lower(row, col) + TILE, :] for col in range(row)]
        strip = jnp.concatenate([tile + tile for tile in tiles] + [triangle + triangle + middle], axis=1)
        product = sum(dot_bf16(change[:, : (row + 1) * TILE], part, NT) for part in pieces_of(strip))
        at = layout.scores + row * chains
        score = packed_ref[at : at + chains, :] - share_ref[:, cols]
        total = total + value[:, cols] * (product - (score + score))
    squares_ref[...] = jnp.broadcast_to(jnp.sum(total, axis=1, keepdims=True), (chains, TILE))


def update_kernel(block, own_ref, other_ref, change_ref, residual_ref, new_ref, x, sems):
    rows = own_ref.shape[1]
    sources, places = [own_ref.at[block], other_ref.at[block]], [x.at[0], x.at[1]]
    start_copies(sources, places, sems, rows)
    for i, start in enumerate(range(0, rows, CHUNK)):
        size = min(CHUNK, rows - start)
        wait_copies(sources, places, sems, i, start, size)
        at = pl.ds(start, size)
        update = dot_bf16(change_ref[0], x[0, at, :], NT) + dot_bf16(change_ref[1], x[1, at, :], NT)
        new_ref[:, at] = residual_ref[:, at] - update


def update(block, genotypes, other, change, residual):
    rows, half = genotypes.shape[1:]
    return pl.pallas_call(
        functools.partial(update_kernel, block),
        out_shape=jax.ShapeDtypeStruct(residual.shape, F32),
        in_specs=[ANY, ANY, VMEM, VMEM],
        out_specs=VMEM,
        scratch_shapes=[
            pltpu.VMEM((2, rows, half), BF16),
            pltpu.SemaphoreType.DMA((-(-rows // CHUNK), 2)),
        ],
        compiler_params=PARAMS,
        cost_estimate=pl.CostEstimate(flops=64 * rows * half * 8, bytes_accessed=4 * rows * half, transcendentals=0),
        name="update",
    )(genotypes, other, change, residual)


def halves_of(shift, core, half):
    change = shift.astype(BF16)
    first, last = change[:, :half], change[:, half:]
    return jnp.where(core == 0, jnp.stack([first, last]), jnp.stack([last, first]))


def line_sums(value, beside, spots):
    stride = 1
    while stride < spots:
        at = [i // stride % LINE for i in range(spots)]
        one, two, three = (
            lax.ppermute(value, "ind", [(i, i + ((at[i] + step) % LINE - at[i]) * stride) for i in range(spots)])
            for step in range(1, LINE)
        )
        if stride == 1:
            one, two, three, beside = lax.optimization_barrier((one, two, three, beside))
        even = lax.axis_index("ind") // stride % 2 == 0
        value = (value + jnp.where(even, three, one)) + (two + jnp.where(even, one, three))
        stride *= LINE
    return value, beside


def local(genotypes, residual, effects, noise, prior_var, block_snps, noise_var, chi_scaled):
    blocks, rows, half = genotypes.shape
    chains = residual.shape[0]
    width = 2 * half
    count = width // TILE
    spots = lax.axis_size("ind")
    core = lax.axis_index("snp")
    core_arg = jnp.reshape(core.astype(jnp.int32), (1,))
    swap = [(0, 1), (1, 0)]
    pieces = -(-rows // CHUNK)

    other = lax.ppermute(genotypes, "snp", swap)
    other_effects = lax.ppermute(effects, "snp", swap)

    layout = Layout(count, chains, spots)
    piece = layout.piece
    square, own_score, own_cross = pl.pallas_call(
        own_kernel,
        out_shape=(
            jax.ShapeDtypeStruct((half, half), F32),
            jax.ShapeDtypeStruct((chains, half), F32),
            jax.ShapeDtypeStruct((half, half), F32),
        ),
        in_specs=[SMEM, ANY, VMEM],
        out_specs=(VMEM,) * 3,
        scratch_shapes=[pltpu.VMEM((2, rows, half), BF16), pltpu.SemaphoreType.DMA((pieces, 2))],
        compiler_params=PARAMS,
        cost_estimate=pl.CostEstimate(flops=2 * rows * half * half, bytes_accessed=2 * rows * half, transcendentals=0),
        name="own",
    )(core_arg, genotypes, residual)
    packed = pl.pallas_call(
        functools.partial(gram_kernel, layout),
        out_shape=jax.ShapeDtypeStruct((spots * piece, TILE), F32),
        in_specs=[SMEM, ANY, ANY, VMEM, VMEM, VMEM],
        out_specs=VMEM,
        scratch_shapes=[
            pltpu.VMEM((rows, width), BF16),
            pltpu.VMEM((half, width), F32),
            pltpu.VMEM((chains, half), F32),
            pltpu.VMEM((chains, 1), F32),
            pltpu.SemaphoreType.DMA((pieces, 2)),
        ],
        compiler_params=PARAMS,
        cost_estimate=pl.CostEstimate(flops=0, bytes_accessed=0, transcendentals=0),
        name="gram",
    )(core_arg, genotypes, other, residual, square, own_score)
    late_other, packed = lax.optimization_barrier((other, packed))
    cross = pl.pallas_call(
        cross_kernel,
        out_shape=jax.ShapeDtypeStruct((2, half, half), F32),
        in_specs=[ANY, ANY, VMEM],
        out_specs=VMEM,
        scratch_shapes=[
            pltpu.VMEM((2, rows, half), BF16),
            pltpu.SemaphoreType.DMA((pieces, 2)),
        ],
        compiler_params=PARAMS,
        cost_estimate=pl.CostEstimate(flops=2 * rows * half * half, bytes_accessed=4 * rows * half, transcendentals=0),
        name="cross",
    )(genotypes, late_other, own_cross)
    packed = lax.all_to_all(packed.reshape(spots, piece, TILE), "ind", 0, 0)
    packed, cross = lax.optimization_barrier((packed, cross))
    packed = jnp.broadcast_to(jnp.sum(packed, axis=0)[None], (spots, piece, TILE))
    packed = lax.all_to_all(packed, "ind", 0, 0).reshape(spots * piece, TILE)

    own_effects = lax.dynamic_index_in_dim(effects, core, 0, keepdims=False)
    got_effects = lax.dynamic_index_in_dim(other_effects, core, 0, keepdims=False)
    block_effects = jnp.where(
        core == 0,
        jnp.concatenate([own_effects, got_effects], axis=1),
        jnp.concatenate([got_effects, own_effects], axis=1),
    )
    block_noise = lax.dynamic_index_in_dim(noise, core, 0, keepdims=False)
    block_rows = lax.dynamic_index_in_dim(block_snps.reshape(blocks, count, TILE), core, 0, keepdims=False)
    scale = jnp.sqrt(noise_var)[:, None]
    factor, inverse, shift = pl.pallas_call(
        functools.partial(factor_kernel, layout),
        out_shape=(
            jax.ShapeDtypeStruct((width + chains, width), F32),
            jax.ShapeDtypeStruct((count, TILE, TILE), F32),
            jax.ShapeDtypeStruct((chains, width), F32),
        ),
        in_specs=[VMEM] * 6,
        out_specs=(VMEM,) * 3,
        scratch_shapes=[pltpu.VMEM((SUB, TILE), F32)],
        compiler_params=PARAMS,
        cost_estimate=pl.CostEstimate(flops=0, bytes_accessed=0, transcendentals=0),
        name="factor",
    )(packed, prior_var.reshape(-1, TILE), block_rows, block_effects, block_noise, scale)

    got_shift = lax.ppermute(shift, "snp", swap)
    share = pl.pallas_call(
        cross_share_kernel,
        out_shape=jax.ShapeDtypeStruct((chains, half), F32),
        in_specs=[SMEM] + [VMEM] * 3,
        out_specs=VMEM,
        compiler_params=PARAMS,
        name="cross_share",
    )(core_arg, shift, got_shift, cross)
    shift_0 = jnp.where(core == 0, shift, got_shift)
    after_0 = update(0, genotypes, other, halves_of(shift_0, core, half), residual)
    share, after_0 = line_sums(share, after_0, spots)
    got = lax.ppermute(share, "snp", swap)
    final, share_all = pl.pallas_call(
        second_kernel,
        out_shape=(jax.ShapeDtypeStruct((chains, width), F32),) * 2,
        in_specs=[SMEM] + [VMEM] * 5,
        out_specs=(VMEM, VMEM),
        compiler_params=PARAMS,
        name="second",
    )(core_arg, shift, share, got, factor, inverse)
    got_final = lax.ppermute(final, "snp", swap)
    added = pl.pallas_call(
        functools.partial(squares_kernel, layout),
        out_shape=jax.ShapeDtypeStruct((chains, TILE), F32),
        in_specs=[VMEM] * 3,
        out_specs=VMEM,
        compiler_params=PARAMS,
        name="squares",
    )(final, share_all, packed)
    got_added = lax.ppermute(added, "snp", swap)
    shift_1 = jnp.where(core == 0, got_final, final)
    new_residual = update(1, genotypes, other, halves_of(shift_1, core, half), after_0)
    squares = packed[layout.squares : layout.used, 0] + (added[:, 0] + got_added[:, 0])
    variance_draw = squares / (rows * spots * chi_scaled)
    own_shift = jnp.stack(
        [lax.dynamic_slice_in_dim(block_shift, core * half, half, 1) for block_shift in (shift_0, shift_1)]
    )
    return (effects + own_shift, new_residual, variance_draw)


def solution(mesh):
    placed = (P(None, "ind", "snp"), P(None, "ind"), P(None, None, "snp"), P(), P(), P(), P(), P())
    return jax.shard_map(
        local,
        mesh=mesh,
        in_specs=placed,
        out_specs=(P(None, None, "snp"), P(None, "ind"), P()),
        check_vma=False,
    )
```

profile of v0, /device:TPU:0, one launch (start us, length us, event | category | flops | bytes accessed | tf_op | source)
XLA Modules:
  0.0 200.5 jit_solution(14014813856190993333)
XLA Ops:
  0.8 1.0 copy-done.1
  1.8 8.2 %own.1 = (f32[512,512]{1,0:T(8,128)S(1)}, f32[32,512]{1,0:T(8,128)S(1)}, f32[512,512]{1,0:T(8,128)}) custom-call(s32[1]{0:T(128)} %bitcast.core_ref, bf16[2,3904,512]{2,1,0:T(8,128)(2,1)} %own_ref.9, f32[32,3904]{1,0:T(8,128)S(1)} %copy-done.1), custom_call_target="tpu_custom_call" | custom-call | flops 2046820352 | bytes 3997696 | tf_op jit(solution)/shard_map/own/pallas_call | solution.py:454
  10.0 3.7 %collective-permute-done.other_ref = bf16[2,3904,512]{2,1,0:T(8,128)(2,1)} collective-permute-done((bf16[2,3904,512]{2,1,0:T(8,128)(2,1)}, bf16[2,3904,512]{2,1,0:T(8,128)(2,1)}, u32[]{:S(2)}, u32[]{:S(2)}) %collective-permute-start) | collective-permute-done | bytes 7995424 | tf_op jit(solution)/shard_map/ppermute | solution.py:449
  13.7 9.7 %gram.1 = f32[4608,128]{1,0:T(8,128)} custom-call(s32[1]{0:T(128)} %bitcast.core_ref, bf16[2,3904,512]{2,1,0:T(8,128)(2,1)} %own_ref.9, bf16[2,3904,512]{2,1,0:T(8,128)(2,1)} %collective-permute-done.other_ref, f32[32,3904]{1,0:T(8,128)S(1)} %copy-done.1, f32[512,512]{1,0:T(8,128)S(1)} %get-tuple-element.19.square_ref, ...), custom_call_target="tpu_custom_call" | custom-call | tf_op jit(solution)/shard_map/gram/pallas_call | solution.py:468
  23.4 11.9 %all-to-all-start = ((f32[64,72,128]{2,1,0:T(8,128)}), f32[64,72,128]{2,1,0:T(8,128)}, u32[]{:S(2)}, u32[]{:S(2)}) async-start(f32[64,72,128]{2,1,0:T(8,128)} %bitcast.28), calls=%async_computation | async-start | bytes 4718592 | tf_op jit(solution)/shard_map/all_to_all | solution.py:498
  35.3 5.9 %cross.1.cross_ref = f32[2,512,512]{2,1,0:T(8,128)} custom-call(bf16[2,3904,512]{2,1,0:T(8,128)(2,1)} %own_ref.9, bf16[2,3904,512]{2,1,0:T(8,128)(2,1)} %collective-permute-done.other_ref, f32[512,512]{1,0:T(8,128)S(1)} %copy-done.3), custom_call_target="tpu_custom_call" | custom-call | flops 2046820352 | bytes 7995392 | tf_op jit(solution)/shard_map/cross/pallas_call | solution.py:485
  41.2 26.7 %all-to-all-done = f32[64,72,128]{2,1,0:T(8,128)} async-done(((f32[64,72,128]{2,1,0:T(8,128)}), f32[64,72,128]{2,1,0:T(8,128)}, u32[]{:S(2)}, u32[]{:S(2)}) %all-to-all-start) | async-done | bytes 2359328 | tf_op jit(solution)/shard_map/all_to_all | solution.py:498
  67.8 1.8 reduce_sum.9
  69.6 1.6 broadcast_in_dim.4
  71.3 7.9 %all-to-all-start.1 = ((f32[64,72,128]{2,1,0:T(8,128)}), f32[64,72,128]{2,1,0:T(8,128)}, u32[]{:S(2)}, u32[]{:S(2)}) async-start(f32[64,72,128]{2,1,0:T(8,128)} %broadcast_in_dim.4), calls=%async_computation.1 | async-start | bytes 4718592 | tf_op jit(solution)/shard_map/all_to_all | solution.py:501
  79.6 1.2 collective-permute-done.1
  80.8 30.6 %all-to-all-done.1 = f32[64,72,128]{2,1,0:T(8,128)} async-done(((f32[64,72,128]{2,1,0:T(8,128)}), f32[64,72,128]{2,1,0:T(8,128)}, u32[]{:S(2)}, u32[]{:S(2)}) %all-to-all-start.1) | async-done | bytes 2359328 | tf_op jit(solution)/shard_map/all_to_all | solution.py:501
  111.4 40.7 %factor.1 = (f32[1056,1024]{1,0:T(8,128)}, f32[8,128,128]{2,1,0:T(8,128)S(1)}, f32[32,1024]{1,0:T(8,128)S(1)}) custom-call(f32[4608,128]{1,0:T(8,128)} %bitcast.2.packed_ref, f32[16,128]{1,0:T(8,128)S(1)} %bitcast.27, s32[8,128]{1,0:T(8,128)S(1)} %dynamic-slice_bitcast_fusion.5.rows_ref, f32[32,1024]{1,0:T(8,128)S(1)} %maximum_select_fusion.effects_ref, ...), custom_call_target="tpu_custom_call" | custom-call | tf_op jit(solution)/shard_map/factor/pallas_call | solution.py:513
  152.1 1.3 collective-permute-done.2.got_ref
  153.5 2.4 %cross_share.1 = f32[32,512]{1,0:T(8,128)S(1)} custom-call(s32[1]{0:T(128)} %bitcast.core_ref, f32[32,1024]{1,0:T(8,128)S(1)} %get-tuple-element.25.shift_ref, f32[32,1024]{1,0:T(8,128)S(1)} %collective-permute-done.2.got_ref, f32[2,512,512]{2,1,0:T(8,128)} %cross.1.cross_ref), custom_call_target="tpu_custom_call" | custom-call | tf_op jit(solution)/shard_map/cross_share/pallas_call | solution.py:529
  155.8 1.2 collective-permute-start.3
  157.0 1.4 collective-permute-start.4
  158.4 2.2 %collective-permute-start.5 = (f32[32,512]{1,0:T(8,128)S(1)}, f32[32,512]{1,0:T(8,128)S(1)}, u32[]{:S(2)}, u32[]{:S(2)}) collective-permute-start(f32[32,512]{1,0:T(8,128)S(1)} %cross_share.1), channel_id=1, source_target_pairs={{0,6},{2,0},{4,2},{6,4},{8,14},{10,8},{12,10},{14,12},{16,22},{18,... | collective-permute-start | bytes 196616 | tf_op jit(solution)/shard_map/ppermute | solution.py:427
  160.6 4.5 %update.2.residual_ref = f32[32,3904]{1,0:T(8,128)S(1)} custom-call(bf16[2,3904,512]{2,1,0:T(8,128)(2,1)} %own_ref.9, bf16[2,3904,512]{2,1,0:T(8,128)(2,1)} %collective-permute-done.other_ref, bf16[2,32,512]{2,1,0:T(8,128)(2,1)S(1)} %maximum_select_fusion.1.change_ref, f32[32,3904]{1,0:T(8,128)S(1)} %copy-done.2), custom_call_target="tpu_custom_call" | custom-call | flops 1023410176 | bytes 7995392 | tf_op jit(solution)/shard_map/update/pallas_call | solution.py:401
  165.2 0.9 collective-permute-start.8
  166.1 0.8 collective-permute-start.7
  166.9 2.4 %collective-permute-start.6 = (f32[32,512]{1,0:T(8,128)S(1)}, f32[32,512]{1,0:T(8,128)S(1)}, u32[]{:S(2)}, u32[]{:S(2)}) collective-permute-start(f32[32,512]{1,0:T(8,128)S(1)} %add_add_fusion.2), channel_id=1, source_target_pairs={{0,24},{2,26},{4,28},{6,30},{8,0},{10,2},{12,4},{14,6},{16,8},{18,... | collective-permute-start | bytes 196616 | tf_op jit(solution)/shard_map/ppermute | solution.py:427
  169.3 1.7 collective-permute-done.8
  171.8 1.9 collective-permute-start.11
  173.8 3.1 %collective-permute-start.9 = (f32[32,512]{1,0:T(8,128)S(1)}, f32[32,512]{1,0:T(8,128)S(1)}, u32[]{:S(2)}, u32[]{:S(2)}) collective-permute-start(f32[32,512]{1,0:T(8,128)S(1)} %add_add_fusion.1), channel_id=1, source_target_pairs={{0,96},{2,98},{4,100},{6,102},{8,104},{10,106},{12,108},{14,110},{... | collective-permute-start | bytes 196616 | tf_op jit(solution)/shard_map/ppermute | solution.py:427
  176.9 0.7 collective-permute-done.11
  177.6 1.5 collective-permute-done.10
  179.2 1.2 collective-permute-done.12.got_ref
  180.5 8.2 %second.1 = (f32[32,1024]{1,0:T(8,128)S(1)}, f32[32,1024]{1,0:T(8,128)S(1)}) custom-call(s32[1]{0:T(128)} %bitcast.core_ref, f32[32,1024]{1,0:T(8,128)S(1)} %get-tuple-element.25.shift_ref, f32[32,512]{1,0:T(8,128)S(1)} %add_add_fusion.share_ref, f32[32,512]{1,0:T(8,128)S(1)} %collective-permute-done.12.got_ref, f32[1056,1024]{1,0:T(8,128)} %get-tuple-element.30.factor_ref, ...), custom_call_target="tpu_custom_call" | custom-call | tf_op jit(solution)/shard_map/second/pallas_call | solution.py:541
  188.7 3.1 %squares.1 = f32[32,128]{1,0:T(8,128)S(1)} custom-call(f32[32,1024]{1,0:T(8,128)S(1)} %get-tuple-element.32.final_ref, f32[32,1024]{1,0:T(8,128)S(1)} %get-tuple-element.34.share_ref, f32[4608,128]{1,0:T(8,128)} %bitcast.2.packed_ref), custom_call_target="tpu_custom_call" | custom-call | tf_op jit(solution)/shard_map/squares/pallas_call | solution.py:550
  192.9 0.8 fusion.1
  195.0 5.3 %update.3 = f32[32,3904]{1,0:T(8,128)} custom-call(bf16[2,3904,512]{2,1,0:T(8,128)(2,1)} %own_ref.9, bf16[2,3904,512]{2,1,0:T(8,128)(2,1)} %collective-permute-done.other_ref, bf16[2,32,512]{2,1,0:T(8,128)(2,1)S(1)} %maximum_select_fusion.2.change_ref, f32[32,3904]{1,0:T(8,128)S(1)} %update.2.residual_ref), custom_call_target="tpu_custom_call" | custom-call | flops 1023410176 | bytes 7995392 | tf_op jit(solution)/shard_map/update/pallas_call | solution.py:401
  (51 shorter events, 4.0 us)
Async XLA Ops:
  0.6 79.0 %copy-start = (f32[2,32,1024]{2,1,0:T(8,128)S(1)}, f32[2,32,1024]{2,1,0:T(8,128)}, u32[]{:S(2)}) copy-start(f32[2,32,1024]{2,1,0:T(8,128)} %param.11) | copy-start | bytes 786436
  0.6 13.0 %collective-permute-start = (bf16[2,3904,512]{2,1,0:T(8,128)(2,1)}, bf16[2,3904,512]{2,1,0:T(8,128)(2,1)}, u32[]{:S(2)}, u32[]{:S(2)}) collective-permute-start(bf16[2,3904,512]{2,1,0:T(8,128)(2,1)} %own_ref.9), channel_id=1, source_target_pairs={{0,1},{1,0},{2,3},{3,2},{4,5},{5,4},{6,7},{7,6},{8,9},{9,8},{10,11... | collective-permute-start | bytes 23986184 | tf_op jit(solution)/shard_map/ppermute | solution.py:449
  0.7 1.0 copy-start.1
  23.4 11.9 %copy-start.3 = (f32[512,512]{1,0:T(8,128)S(1)}, f32[512,512]{1,0:T(8,128)}, u32[]{:S(2)}) copy-start(f32[512,512]{1,0:T(8,128)} %get-tuple-element.23.own_cross_ref) | copy-start | bytes 3145732
  23.4 44.4 %all-to-all-start = ((f32[64,72,128]{2,1,0:T(8,128)}), f32[64,72,128]{2,1,0:T(8,128)}, u32[]{:S(2)}, u32[]{:S(2)}) async-start(f32[64,72,128]{2,1,0:T(8,128)} %bitcast.28), calls=%async_computation | async-start | bytes 4718592 | tf_op jit(solution)/shard_map/all_to_all | solution.py:498
  71.3 7.9 %copy-start.5 = (f32[2,32,512]{2,1,0:T(8,128)S(1)}, f32[2,32,512]{2,1,0:T(8,128)}, u32[]{:S(2)}) copy-start(f32[2,32,512]{2,1,0:T(8,128)} %param.10) | copy-start | bytes 393220
  71.3 8.2 %copy-start.7 = (f32[32]{0:T(128)S(1)}, f32[32]{0:T(128)}, u32[]{:S(2)}) copy-start(f32[32]{0:T(128)} %param.14) | copy-start | bytes 388
  71.3 8.2 %copy-start.6 = (s32[2048]{0:T(1024)S(1)}, s32[2048]{0:T(1024)}, u32[]{:S(2)}) copy-start(s32[2048]{0:T(1024)} %param.13) | copy-start | bytes 24580
  71.3 40.1 %copy-start.4 = (f32[2048]{0:T(1024)S(1)}, f32[2048]{0:T(1024)}, u32[]{:S(2)}) copy-start(f32[2048]{0:T(1024)} %param.12) | copy-start | bytes 24580
  71.3 40.1 %all-to-all-start.1 = ((f32[64,72,128]{2,1,0:T(8,128)}), f32[64,72,128]{2,1,0:T(8,128)}, u32[]{:S(2)}, u32[]{:S(2)}) async-start(f32[64,72,128]{2,1,0:T(8,128)} %broadcast_in_dim.4), calls=%async_computation.1 | async-start | bytes 4718592 | tf_op jit(solution)/shard_map/all_to_all | solution.py:501
  79.2 1.6 collective-permute-start.1
  111.4 49.2 %copy-start.2 = (f32[32,3904]{1,0:T(8,128)S(1)}, f32[32,3904]{1,0:T(8,128)}, u32[]{:S(2)}) copy-start(f32[32,3904]{1,0:T(8,128)} %residual_ref.5) | copy-start | bytes 1499140
  152.1 1.3 collective-permute-start.2
  155.8 9.3 %collective-permute-start.3 = (f32[32,512]{1,0:T(8,128)S(1)}, f32[32,512]{1,0:T(8,128)S(1)}, u32[]{:S(2)}, u32[]{:S(2)}) collective-permute-start(f32[32,512]{1,0:T(8,128)S(1)} %cross_share.1), channel_id=1, source_target_pairs={{0,2},{2,4},{4,6},{6,0},{8,10},{10,12},{12,14},{14,8},{16,18},{18,... | collective-permute-start | bytes 196616 | tf_op jit(solution)/shard_map/ppermute | solution.py:427
  157.0 8.1 %collective-permute-start.4 = (f32[32,512]{1,0:T(8,128)S(1)}, f32[32,512]{1,0:T(8,128)S(1)}, u32[]{:S(2)}, u32[]{:S(2)}) collective-permute-start(f32[32,512]{1,0:T(8,128)S(1)} %cross_share.1), channel_id=1, source_target_pairs={{0,4},{2,6},{4,0},{6,2},{8,12},{10,14},{12,8},{14,10},{16,20},{18,... | collective-permute-start | bytes 196616 | tf_op jit(solution)/shard_map/ppermute | solution.py:427
  158.4 6.8 %collective-permute-start.5 = (f32[32,512]{1,0:T(8,128)S(1)}, f32[32,512]{1,0:T(8,128)S(1)}, u32[]{:S(2)}, u32[]{:S(2)}) collective-permute-start(f32[32,512]{1,0:T(8,128)S(1)} %cross_share.1), channel_id=1, source_target_pairs={{0,6},{2,0},{4,2},{6,4},{8,14},{10,8},{12,10},{14,12},{16,22},{18,... | collective-permute-start | bytes 196616 | tf_op jit(solution)/shard_map/ppermute | solution.py:427
  165.2 5.9 %collective-permute-start.8 = (f32[32,512]{1,0:T(8,128)S(1)}, f32[32,512]{1,0:T(8,128)S(1)}, u32[]{:S(2)}, u32[]{:S(2)}) collective-permute-start(f32[32,512]{1,0:T(8,128)S(1)} %add_add_fusion.2), channel_id=1, source_target_pairs={{0,16},{2,18},{4,20},{6,22},{8,24},{10,26},{12,28},{14,30},{16,0},... | collective-permute-start | bytes 196616 | tf_op jit(solution)/shard_map/ppermute | solution.py:427
  166.1 5.7 %collective-permute-start.7 = (f32[32,512]{1,0:T(8,128)S(1)}, f32[32,512]{1,0:T(8,128)S(1)}, u32[]{:S(2)}, u32[]{:S(2)}) collective-permute-start(f32[32,512]{1,0:T(8,128)S(1)} %add_add_fusion.2), channel_id=1, source_target_pairs={{0,8},{2,10},{4,12},{6,14},{8,16},{10,18},{12,20},{14,22},{16,24},... | collective-permute-start | bytes 196616 | tf_op jit(solution)/shard_map/ppermute | solution.py:427
  166.9 4.9 %collective-permute-start.6 = (f32[32,512]{1,0:T(8,128)S(1)}, f32[32,512]{1,0:T(8,128)S(1)}, u32[]{:S(2)}, u32[]{:S(2)}) collective-permute-start(f32[32,512]{1,0:T(8,128)S(1)} %add_add_fusion.2), channel_id=1, source_target_pairs={{0,24},{2,26},{4,28},{6,30},{8,0},{10,2},{12,4},{14,6},{16,8},{18,... | collective-permute-start | bytes 196616 | tf_op jit(solution)/shard_map/ppermute | solution.py:427
  171.8 5.8 %collective-permute-start.11 = (f32[32,512]{1,0:T(8,128)S(1)}, f32[32,512]{1,0:T(8,128)S(1)}, u32[]{:S(2)}, u32[]{:S(2)}) collective-permute-start(f32[32,512]{1,0:T(8,128)S(1)} %add_add_fusion.1), channel_id=1, source_target_pairs={{0,64},{2,66},{4,68},{6,70},{8,72},{10,74},{12,76},{14,78},{16,80}... | collective-permute-start | bytes 196616 | tf_op jit(solution)/shard_map/ppermute | solution.py:427
  173.6 5.5 %collective-permute-start.10 = (f32[32,512]{1,0:T(8,128)S(1)}, f32[32,512]{1,0:T(8,128)S(1)}, u32[]{:S(2)}, u32[]{:S(2)}) collective-permute-start(f32[32,512]{1,0:T(8,128)S(1)} %add_add_fusion.1), channel_id=1, source_target_pairs={{0,32},{2,34},{4,36},{6,38},{8,40},{10,42},{12,44},{14,46},{16,48}... | collective-permute-start | bytes 196616 | tf_op jit(solution)/shard_map/ppermute | solution.py:427
  173.8 5.3 %collective-permute-start.9 = (f32[32,512]{1,0:T(8,128)S(1)}, f32[32,512]{1,0:T(8,128)S(1)}, u32[]{:S(2)}, u32[]{:S(2)}) collective-permute-start(f32[32,512]{1,0:T(8,128)S(1)} %add_add_fusion.1), channel_id=1, source_target_pairs={{0,96},{2,98},{4,100},{6,102},{8,104},{10,106},{12,108},{14,110},{... | collective-permute-start | bytes 196616 | tf_op jit(solution)/shard_map/ppermute | solution.py:427
  179.1 1.3 collective-permute-start.12
  188.7 5.1 %copy-start.8 = (f32[32]{0:T(128)S(1)}, f32[32]{0:T(128)}, u32[]{:S(2)}) copy-start(f32[32]{0:T(128)} %param.15) | copy-start | bytes 388
  191.7 1.2 collective-permute-start.14
  191.9 2.4 %collective-permute-start.13 = (f32[32,1024]{1,0:T(8,128)S(1)}, f32[32,1024]{1,0:T(8,128)S(1)}, u32[]{:S(2)}, u32[]{:S(2)}) collective-permute-start(f32[32,1024]{1,0:T(8,128)S(1)} %get-tuple-element.32.final_ref), channel_id=1, source_target_pairs={{0,1},{1,0},{2,3},{3,2},{4,5},{5,4},{6,7},{7,6},{8,9},{9,8},{10,11... | collective-permute-start | bytes 393224 | tf_op jit(solution)/shard_map/ppermute | solution.py:549
where the time goes:
time: 202 us; the launch traced here: 201 us
  Pallas kernels  88 us (44%)
  waiting for transfers between devices  70 us (35%)
  starting transfers between devices  34.6 us (17%)
  other arithmetic  3.98 us (2%)
  local copies, waits for them, and re-layouts  2.85 us (1%)
    pallas_call x1, Pallas kernels, local(): pl.pallas_call(functools.partial(factor_kernel, layout), out_shape=(jax.S...  40.7 us
    all_to_all x1, waiting for transfers between devices, local(): packed = lax.all_to_all(packed, 'ind', 0, 0).reshape(spots * piece, TILE)  30.6 us
    all_to_all x1, waiting for transfers between devices, local(): packed = lax.all_to_all(packed.reshape(spots, piece, TILE), 'ind', 0, 0)  26.7 us
    ppermute x9, starting transfers between devices, line_sums(): lax.ppermute(value, 'ind', [(i, i + ((at[i] + step) % LINE - at[i]) * str...  13.9 us
    all_to_all x1, starting transfers between devices, local(): packed = lax.all_to_all(packed.reshape(spots, piece, TILE), 'ind', 0, 0)  11.9 us
    pallas_call x2, Pallas kernels, update(): pl.pallas_call(functools.partial(update_kernel, block), out_shape=jax.Sha...  9.81 us
    pallas_call x1, Pallas kernels, local(): pl.pallas_call(functools.partial(gram_kernel, layout), out_shape=jax.Shap...  9.71 us
    pallas_call x1, Pallas kernels, local(): pl.pallas_call(own_kernel, out_shape=(jax.ShapeDtypeStruct((half, half),...  8.22 us
  transfers between devices with their start and end apart: 17, of which 11 were waited for; matrix products, arithmetic and copies ran while one was open for 1% of the time, Pallas kernels for 9%

commit v1 on v0

--- a/solution.py
+++ b/solution.py
@@ -252,6 +252,30 @@
     packed_ref[layout.used :, :] = jnp.zeros((layout.rows - layout.used, TILE), F32)
 
 
+def sum_kernel(parts_ref, sums_ref, parts, copies, in_sems, out_sems):
+    count, each = parts.shape[0], copies.shape[0]
+    moves = [
+        pltpu.make_async_copy(parts_ref.at[i : i + each], parts.at[i : i + each], in_sems.at[i // each])
+        for i in range(0, count, each)
+    ]
+    for move in moves:
+        move.start()
+    total = None
+    for i, move in enumerate(moves):
+        move.wait()
+        group = tree_sum([parts[i * each + j] for j in range(each)])
+        total = group if total is None else total + group
+    for i in range(each):
+        copies[i] = total
+    moves = [
+        pltpu.make_async_copy(copies, sums_ref.at[i : i + each], out_sems.at[i // each]) for i in range(0, count, each)
+    ]
+    for move in moves:
+        move.start()
+    for move in moves:
+        move.wait()
+
+
 def cross_kernel(own_ref, other_ref, own_cross_ref, cross_ref, x, sems):
     rows = own_ref.shape[1]
     sources, places = [other_ref.at[0], own_ref.at[1]], [x.at[0], x.at[1]]
@@ -267,19 +291,25 @@
     chunk_loop(rows, body)
 
 
-def backward(moved, factor_ref, inverse_ref, count):
-    solved = [None] * count
-    for k in reversed(range(count)):
+def panel_rows(width, k):
+    start = sum(width - j * STRIP for j in range(1, k + 1))
+    return slice(start, start + width - (k + 1) * STRIP)
+
+
+def backward(moved, panels_ref, inverse_ref):
+    width = len(moved) * STRIP
+    solved = [None] * len(moved)
+    for k in reversed(range(len(moved))):
         solved[k] = dot_rows(moved[k], inverse_ref[k], NN)
         if k:
-            share = dot_rows(solved[k], factor_ref[k * TILE : k * TILE + TILE, : k * TILE], NN)
             for j in range(k):
-                moved[j] = moved[j] - share[:, j * TILE : j * TILE + TILE]
+                at = panel_rows(width, j).start + (k - j - 1) * STRIP
+                moved[j] = moved[j] - dot_rows(solved[k], panels_ref[at : at + STRIP, :], NN)
     return solved
 
 
 def factor_kernel(
-    layout, packed_ref, prior_ref, rows_ref, effects_ref, noise_ref, scale_ref, factor_ref, inverse_ref, shift_ref, zero_ref
+    layout, packed_ref, prior_ref, rows_ref, effects_ref, noise_ref, scale_ref, panels_ref, inverse_ref, shift_ref, factor_ref, zero_ref
 ):
     width = factor_ref.shape[1]
     count = width // TILE
@@ -310,29 +340,38 @@
     @pl.loop(0, count)
     def _(k):
         at = pl.multiple_of(k * TILE, TILE)
-        inverse_ref[k] = inverse_factor(factor_ref[pl.ds(at, TILE), pl.ds(at, TILE)], zero_ref[...])
+        pair, side = lax.shift_right_logical(k, 1), pl.ds(pl.multiple_of(lax.bitwise_and(k, 1) * TILE, TILE), TILE)
+        inverse_ref[pair, side, side] = inverse_factor(factor_ref[pl.ds(at, TILE), pl.ds(at, TILE)], zero_ref[...])
         for step in range(count):
 
             @pl.when(k == step)
             def _():
-                lo = (step + 1) * TILE
-                factor_ref[lo:, step * TILE : lo] = dot_exact(factor_ref[lo:, step * TILE : lo], inverse_ref[step], NT)
+                lo, hi = step * TILE, (step + 1) * TILE
+                side = slice(step % 2 * TILE, step % 2 * TILE + TILE)
+                inverse = inverse_ref[step // 2, side, side]
+                factor_ref[hi:, lo:hi] = dot_exact(factor_ref[hi:, lo:hi], inverse, NT)
                 if step % 2 == 0:
-                    panel = factor_ref[lo:, step * TILE : lo]
-                    factor_ref[lo:, lo : lo + TILE] = factor_ref[lo:, lo : lo + TILE] - dot_exact(panel, panel[:TILE, :], NT)
+                    panel = factor_ref[hi:, lo:hi]
+                    factor_ref[hi:, hi : hi + TILE] = factor_ref[hi:, hi : hi + TILE] - dot_exact(panel, panel[:TILE, :], NT)
                 else:
-                    for c in range(lo, width, STRIP):
-                        end = min(c + STRIP, width)
-                        panel = factor_ref[c:, (step - 1) * TILE : lo]
-                        factor_ref[c:, c:end] = factor_ref[c:, c:end] - dot_exact(panel, panel[: end - c, :], NT)
+                    for c in range(hi, width, STRIP):
+                        panel = factor_ref[c:, lo - TILE : hi]
+                        factor_ref[c:, c : c + STRIP] = factor_ref[c:, c : c + STRIP] - dot_exact(
+                            panel, panel[:STRIP, :], NT
+                        )
+                    below = dot_exact(factor_ref[lo:hi, lo - TILE : lo], inverse_ref[step // 2, :TILE, :TILE], NN)
+                    inverse_ref[step // 2, TILE:, :TILE] = -dot_exact(inverse, below, NN)
+                    inverse_ref[step // 2, :TILE, TILE:] = jnp.zeros((TILE, TILE), F32)
 
     scale = scale_ref[...]
     moved = [
-        factor_ref[width : width + chains, j * TILE : j * TILE + TILE] + scale * noise_ref[:, j * TILE : j * TILE + TILE]
-        for j in range(count)
+        factor_ref[width : width + chains, j : j + STRIP] + scale * noise_ref[:, j : j + STRIP]
+        for j in range(0, width, STRIP)
     ]
-    for j, part in enumerate(backward(moved, factor_ref, inverse_ref, count)):
-        shift_ref[:, j * TILE : j * TILE + TILE] = part
+    for k in range(width // STRIP - 1):
+        panels_ref[panel_rows(width, k), :] = factor_ref[(k + 1) * STRIP : width, k * STRIP : (k + 1) * STRIP]
+    for j, part in enumerate(backward(moved, panels_ref, inverse_ref)):
+        shift_ref[:, j * STRIP : j * STRIP + STRIP] = part
 
 
 def cross_share_kernel(core_ref, shift_ref, got_ref, cross_ref, share_ref):
@@ -348,28 +387,22 @@
     )
 
 
-def second_kernel(core_ref, shift_ref, share_ref, got_ref, factor_ref, inverse_ref, final_ref, share_all_ref):
-    width = factor_ref.shape[1]
-    count = width // TILE
+def second_kernel(layout, core_ref, shift_ref, share_ref, got_ref, panels_ref, inverse_ref, packed_ref, final_ref):
+    width, count, chains = shift_ref.shape[1], layout.count, layout.chains
     keep = jnp.where(core_ref[0] == 1, 1.0, 0.0)
     right = jnp.concatenate([got_ref[...], share_ref[...]], axis=1) * keep
-    share_all_ref[...] = right
-    moved = [right[:, j * TILE : j * TILE + TILE] for j in range(count)]
-    for k in range(count):
+    moved = [right[:, j : j + STRIP] for j in range(0, width, STRIP)]
+    for k in range(len(moved)):
         moved[k] = dot_rows(moved[k], inverse_ref[k], NT)
-        lo = (k + 1) * TILE
+        lo = (k + 1) * STRIP
         if lo < width:
-            change_by = dot_rows(moved[k], factor_ref[lo:width, k * TILE : lo], NT)
-            for j in range(k + 1, count):
-                moved[j] = moved[j] - change_by[:, (j - k - 1) * TILE : (j - k) * TILE]
-    for j, part in enumerate(backward(moved, factor_ref, inverse_ref, count)):
-        cols = slice(j * TILE, j * TILE + TILE)
+            change_by = dot_rows(moved[k], panels_ref[panel_rows(width, k), :], NT)
+            for j in range(k + 1, len(moved)):
+                moved[j] = moved[j] - change_by[:, (j - k - 1) * STRIP : (j - k) * STRIP]
+    for j, part in enumerate(backward(moved, panels_ref, inverse_ref)):
+        cols = slice(j * STRIP, j * STRIP + STRIP)
         final_ref[:, cols] = shift_ref[:, cols] - part
-
-
-def squares_kernel(layout, final_ref, share_ref, packed_ref, squares_ref):
-    count, chains = layout.count, layout.chains
-    change = final_ref[...].astype(BF16)
+    change = final_ref[:, :width].astype(BF16)
     value = change.astype(F32)
     total = jnp.zeros((chains, TILE), F32)
     for row in range(count):
@@ -379,44 +412,61 @@
         strip = jnp.concatenate([tile + tile for tile in tiles] + [triangle + triangle + middle], axis=1)
         product = sum(dot_bf16(change[:, : (row + 1) * TILE], part, NT) for part in pieces_of(strip))
         at = layout.scores + row * chains
-        score = packed_ref[at : at + chains, :] - share_ref[:, cols]
+        score = packed_ref[at : at + chains, :] - right[:, cols]
         total = total + value[:, cols] * (product - (score + score))
-    squares_ref[...] = jnp.broadcast_to(jnp.sum(total, axis=1, keepdims=True), (chains, TILE))
-
-
-def update_kernel(block, own_ref, other_ref, change_ref, residual_ref, new_ref, x, sems):
-    rows = own_ref.shape[1]
+    final_ref[:, width:] = jnp.broadcast_to(jnp.sum(total, axis=1, keepdims=True), (chains, TILE))
+
+
+def update_rows(block, core, own_ref, other_ref, shift, residual_ref, new_ref, x, sems):
+    rows, half = own_ref.shape[1:]
     sources, places = [own_ref.at[block], other_ref.at[block]], [x.at[0], x.at[1]]
     start_copies(sources, places, sems, rows)
+    mine = jnp.where(core == 0, shift[:, :half], shift[:, half:])
+    theirs = jnp.where(core == 0, shift[:, half:], shift[:, :half])
+    own_change, their_change = mine.astype(BF16), theirs.astype(BF16)
     for i, start in enumerate(range(0, rows, CHUNK)):
         size = min(CHUNK, rows - start)
         wait_copies(sources, places, sems, i, start, size)
         at = pl.ds(start, size)
-        update = dot_bf16(change_ref[0], x[0, at, :], NT) + dot_bf16(change_ref[1], x[1, at, :], NT)
-        new_ref[:, at] = residual_ref[:, at] - update
-
-
-def update(block, genotypes, other, change, residual):
+        change = dot_bf16(own_change, x[0, at, :], NT) + dot_bf16(their_change, x[1, at, :], NT)
+        new_ref[:, at] = residual_ref[:, at] - change
+    return mine
+
+
+def first_update_kernel(core_ref, own_ref, other_ref, here_ref, there_ref, residual_ref, new_ref, mine_ref, x, sems):
+    core = core_ref[0]
+    shift = jnp.where(core == 0, here_ref[...], there_ref[...])
+    mine_ref[...] = update_rows(0, core, own_ref, other_ref, shift, residual_ref, new_ref, x, sems)
+
+
+def last_update_kernel(
+    layout, people, core_ref, own_ref, other_ref, here_ref, there_ref, residual_ref, effects_ref, first_ref, norm_ref,
+    chi_ref, new_ref, new_effects_ref, draw_ref, x, sems
+):
+    core, width = core_ref[0], 2 * own_ref.shape[2]
+    squares = norm_ref[...] + (here_ref[:, width:] + there_ref[:, width:])
+    draw_ref[...] = squares.T[:1, :] / (people * chi_ref[...])
+    shift = jnp.where(core == 1, here_ref[:, :width], there_ref[:, :width])
+    mine = update_rows(1, core, own_ref, other_ref, shift, residual_ref, new_ref, x, sems)
+    new_effects_ref[0] = effects_ref[0] + first_ref[...]
+    new_effects_ref[1] = effects_ref[1] + mine
+
+
+def update_call(kernel, out_shape, genotypes, name, *operands):
     rows, half = genotypes.shape[1:]
     return pl.pallas_call(
-        functools.partial(update_kernel, block),
-        out_shape=jax.ShapeDtypeStruct(residual.shape, F32),
-        in_specs=[ANY, ANY, VMEM, VMEM],
-        out_specs=VMEM,
+        kernel,
+        out_shape=out_shape,
+        in_specs=[SMEM, ANY, ANY] + [VMEM] * (len(operands) - 2),
+        out_specs=(VMEM,) * len(out_shape),
         scratch_shapes=[
             pltpu.VMEM((2, rows, half), BF16),
             pltpu.SemaphoreType.DMA((-(-rows // CHUNK), 2)),
         ],
         compiler_params=PARAMS,
         cost_estimate=pl.CostEstimate(flops=64 * rows * half * 8, bytes_accessed=4 * rows * half, transcendentals=0),
-        name="update",
-    )(genotypes, other, change, residual)
-
-
-def halves_of(shift, core, half):
-    change = shift.astype(BF16)
-    first, last = change[:, :half], change[:, half:]
-    return jnp.where(core == 0, jnp.stack([first, last]), jnp.stack([last, first]))
+        name=name,
+    )(operands[0], genotypes, *operands[1:])
 
 
 def line_sums(value, beside, spots):
@@ -497,7 +547,20 @@
     )(genotypes, late_other, own_cross)
     packed = lax.all_to_all(packed.reshape(spots, piece, TILE), "ind", 0, 0)
     packed, cross = lax.optimization_barrier((packed, cross))
-    packed = jnp.broadcast_to(jnp.sum(packed, axis=0)[None], (spots, piece, TILE))
+    packed = pl.pallas_call(
+        sum_kernel,
+        out_shape=jax.ShapeDtypeStruct(packed.shape, F32),
+        in_specs=[ANY],
+        out_specs=ANY,
+        scratch_shapes=[
+            pltpu.VMEM((spots, piece, TILE), F32),
+            pltpu.VMEM((SUB, piece, TILE), F32),
+            pltpu.SemaphoreType.DMA((spots // SUB,)),
+            pltpu.SemaphoreType.DMA((spots // SUB,)),
+        ],
+        compiler_params=PARAMS,
+        name="sums",
+    )(packed)
     packed = lax.all_to_all(packed, "ind", 0, 0).reshape(spots * piece, TILE)
 
     own_effects = lax.dynamic_index_in_dim(effects, core, 0, keepdims=False)
@@ -510,16 +573,16 @@
     block_noise = lax.dynamic_index_in_dim(noise, core, 0, keepdims=False)
     block_rows = lax.dynamic_index_in_dim(block_snps.reshape(blocks, count, TILE), core, 0, keepdims=False)
     scale = jnp.sqrt(noise_var)[:, None]
-    factor, inverse, shift = pl.pallas_call(
+    panels, inverse, shift = pl.pallas_call(
         functools.partial(factor_kernel, layout),
         out_shape=(
-            jax.ShapeDtypeStruct((width + chains, width), F32),
-            jax.ShapeDtypeStruct((count, TILE, TILE), F32),
+            jax.ShapeDtypeStruct((panel_rows(width, width // STRIP - 1).start, STRIP), F32),
+            jax.ShapeDtypeStruct((width // STRIP, STRIP, STRIP), F32),
             jax.ShapeDtypeStruct((chains, width), F32),
         ),
         in_specs=[VMEM] * 6,
         out_specs=(VMEM,) * 3,
-        scratch_shapes=[pltpu.VMEM((SUB, TILE), F32)],
+        scratch_shapes=[pltpu.VMEM((width + chains, width), F32), pltpu.VMEM((SUB, TILE), F32)],
         compiler_params=PARAMS,
         cost_estimate=pl.CostEstimate(flops=0, bytes_accessed=0, transcendentals=0),
         name="factor",
@@ -534,36 +597,48 @@
         compiler_params=PARAMS,
         name="cross_share",
     )(core_arg, shift, got_shift, cross)
-    shift_0 = jnp.where(core == 0, shift, got_shift)
-    after_0 = update(0, genotypes, other, halves_of(shift_0, core, half), residual)
+    after_0, first_shift = update_call(
+        first_update_kernel,
+        (jax.ShapeDtypeStruct(residual.shape, F32), jax.ShapeDtypeStruct((chains, half), F32)),
+        genotypes,
+        "first_update",
+        core_arg,
+        other,
+        shift,
+        got_shift,
+        residual,
+    )
     share, after_0 = line_sums(share, after_0, spots)
     got = lax.ppermute(share, "snp", swap)
-    final, share_all = pl.pallas_call(
-        second_kernel,
-        out_shape=(jax.ShapeDtypeStruct((chains, width), F32),) * 2,
-        in_specs=[SMEM] + [VMEM] * 5,
-        out_specs=(VMEM, VMEM),
+    final = pl.pallas_call(
+        functools.partial(second_kernel, layout),
+        out_shape=jax.ShapeDtypeStruct((chains, width + TILE), F32),
+        in_specs=[SMEM] + [VMEM] * 6,
+        out_specs=VMEM,
         compiler_params=PARAMS,
         name="second",
-    )(core_arg, shift, share, got, factor, inverse)
+    )(core_arg, shift, share, got, panels, inverse, packed)
     got_final = lax.ppermute(final, "snp", swap)
-    added = pl.pallas_call(
-        functools.partial(squares_kernel, layout),
-        out_shape=jax.ShapeDtypeStruct((chains, TILE), F32),
-        in_specs=[VMEM] * 3,
-        out_specs=VMEM,
-        compiler_params=PARAMS,
-        name="squares",
-    )(final, share_all, packed)
-    got_added = lax.ppermute(added, "snp", swap)
-    shift_1 = jnp.where(core == 0, got_final, final)
-    new_residual = update(1, genotypes, other, halves_of(shift_1, core, half), after_0)
-    squares = packed[layout.squares : layout.used, 0] + (added[:, 0] + got_added[:, 0])
-    variance_draw = squares / (rows * spots * chi_scaled)
-    own_shift = jnp.stack(
-        [lax.dynamic_slice_in_dim(block_shift, core * half, half, 1) for block_shift in (shift_0, shift_1)]
+    new_residual, new_effects, draw = update_call(
+        functools.partial(last_update_kernel, layout, rows * spots),
+        (
+            jax.ShapeDtypeStruct(residual.shape, F32),
+            jax.ShapeDtypeStruct(effects.shape, F32),
+            jax.ShapeDtypeStruct((1, chains), F32),
+        ),
+        genotypes,
+        "last_update",
+        core_arg,
+        other,
+        final,
+        got_final,
+        after_0,
+        effects,
+        first_shift,
+        packed[layout.squares : layout.used],
+        chi_scaled[None, :],
     )
-    return (effects + own_shift, new_residual, variance_draw)
+    return (new_effects, new_residual, draw[0])
 
 
 def solution(mesh):

time: 202 us -> 194 us (0.960)
  other arithmetic: 3.98 us -> 0.08 us
  Pallas kernels: 88 us -> 85.7 us
  transfers between devices with their start and end apart: 17 -> 16, of which waited for: 11 -> 11; matrix products, arithmetic and copies ran while one was open for 1% -> 0% of each run, Pallas kernels for 9% -> 10%
where the time goes in v1:
time: 194 us; the launch traced here: 193 us
  Pallas kernels  85.7 us (44%)
  waiting for transfers between devices  69.8 us (36%)
  starting transfers between devices  34.1 us (18%)
    pallas_call x1, Pallas kernels, local(): pl.pallas_call(functools.partial(factor_kernel, layout), out_shape=(jax.S...  39.3 us
    all_to_all x1, waiting for transfers between devices, local(): packed = lax.all_to_all(packed, 'ind', 0, 0).reshape(spots * piece, TILE)  30.6 us
    all_to_all x1, waiting for transfers between devices, local(): packed = lax.all_to_all(packed.reshape(spots, piece, TILE), 'ind', 0, 0)  26.7 us
    ppermute x9, starting transfers between devices, line_sums(): lax.ppermute(value, 'ind', [(i, i + ((at[i] + step) % LINE - at[i]) * str...  13.7 us
    all_to_all x1, starting transfers between devices, local(): packed = lax.all_to_all(packed.reshape(spots, piece, TILE), 'ind', 0, 0)  11.9 us
    pallas_call x2, Pallas kernels, update_call(): pl.pallas_call(kernel, out_shape=out_shape, in_specs=[SMEM, ANY, ANY] + [...  9.81 us
    pallas_call x1, Pallas kernels, local(): pl.pallas_call(functools.partial(gram_kernel, layout), out_shape=jax.Shap...  9.71 us
    pallas_call x1, Pallas kernels, local(): pl.pallas_call(own_kernel, out_shape=(jax.ShapeDtypeStruct((half, half),...  8.22 us
  transfers between devices with their start and end apart: 16, of which 11 were waited for; matrix products, arithmetic and copies ran while one was open for 0% of the time, Pallas kernels for 10%

profile of v1, /device:TPU:0, one launch (start us, length us, event | category | flops | bytes accessed | tf_op | source)
XLA Modules:
  0.0 192.7 jit_solution(7798046014401092053)
XLA Ops:
  0.8 1.0 copy-done.1
  1.8 8.2 %own.1 = (f32[512,512]{1,0:T(8,128)S(1)}, f32[32,512]{1,0:T(8,128)S(1)}, f32[512,512]{1,0:T(8,128)}) custom-call(s32[1]{0:T(128)} %bitcast.core_ref, bf16[2,3904,512]{2,1,0:T(8,128)(2,1)} %own_ref.9, f32[32,3904]{1,0:T(8,128)S(1)} %copy-done.1), custom_call_target="tpu_custom_call" | custom-call | flops 2046820352 | bytes 3997696 | tf_op jit(solution)/shard_map/own/pallas_call | solution.py:504
  10.0 3.7 %collective-permute-done.other_ref = bf16[2,3904,512]{2,1,0:T(8,128)(2,1)} collective-permute-done((bf16[2,3904,512]{2,1,0:T(8,128)(2,1)}, bf16[2,3904,512]{2,1,0:T(8,128)(2,1)}, u32[]{:S(2)}, u32[]{:S(2)}) %collective-permute-start) | collective-permute-done | bytes 7995424 | tf_op jit(solution)/shard_map/ppermute | solution.py:499
  13.7 9.7 %gram.1 = f32[4608,128]{1,0:T(8,128)} custom-call(s32[1]{0:T(128)} %bitcast.core_ref, bf16[2,3904,512]{2,1,0:T(8,128)(2,1)} %own_ref.9, bf16[2,3904,512]{2,1,0:T(8,128)(2,1)} %collective-permute-done.other_ref, f32[32,3904]{1,0:T(8,128)S(1)} %copy-done.1, f32[512,512]{1,0:T(8,128)S(1)} %get-tuple-element.22.square_ref, ...), custom_call_target="tpu_custom_call" | custom-call | tf_op jit(solution)/shard_map/gram/pallas_call | solution.py:518
  23.4 11.9 %all-to-all-start = ((f32[64,72,128]{2,1,0:T(8,128)}), f32[64,72,128]{2,1,0:T(8,128)}, u32[]{:S(2)}, u32[]{:S(2)}) async-start(f32[64,72,128]{2,1,0:T(8,128)} %bitcast.19), calls=%async_computation | async-start | bytes 4718592 | tf_op jit(solution)/shard_map/all_to_all | solution.py:548
  35.3 5.9 %cross.1.cross_ref = f32[2,512,512]{2,1,0:T(8,128)} custom-call(bf16[2,3904,512]{2,1,0:T(8,128)(2,1)} %own_ref.9, bf16[2,3904,512]{2,1,0:T(8,128)(2,1)} %collective-permute-done.other_ref, f32[512,512]{1,0:T(8,128)S(1)} %copy-done.3), custom_call_target="tpu_custom_call" | custom-call | flops 2046820352 | bytes 7995392 | tf_op jit(solution)/shard_map/cross/pallas_call | solution.py:535
  41.2 26.7 %all-to-all-done.parts_ref = f32[64,72,128]{2,1,0:T(8,128)} async-done(((f32[64,72,128]{2,1,0:T(8,128)}), f32[64,72,128]{2,1,0:T(8,128)}, u32[]{:S(2)}, u32[]{:S(2)}) %all-to-all-start) | async-done | bytes 2359328 | tf_op jit(solution)/shard_map/all_to_all | solution.py:548
  67.8 3.2 %sums.1 = f32[64,72,128]{2,1,0:T(8,128)} custom-call(f32[64,72,128]{2,1,0:T(8,128)} %all-to-all-done.parts_ref), custom_call_target="tpu_custom_call" | custom-call | tf_op jit(solution)/shard_map/sums/pallas_call | solution.py:550
  71.1 7.9 %all-to-all-start.1 = ((f32[64,72,128]{2,1,0:T(8,128)}), f32[64,72,128]{2,1,0:T(8,128)}, u32[]{:S(2)}, u32[]{:S(2)}) async-start(f32[64,72,128]{2,1,0:T(8,128)} %sums.1), calls=%async_computation.1 | async-start | bytes 4718592 | tf_op jit(solution)/shard_map/all_to_all | solution.py:564
  79.4 1.2 collective-permute-done.1
  80.6 30.6 %all-to-all-done.1 = f32[64,72,128]{2,1,0:T(8,128)} async-done(((f32[64,72,128]{2,1,0:T(8,128)}), f32[64,72,128]{2,1,0:T(8,128)}, u32[]{:S(2)}, u32[]{:S(2)}) %all-to-all-start.1) | async-done | bytes 2359328 | tf_op jit(solution)/shard_map/all_to_all | solution.py:564
  111.2 39.3 %factor.1 = (f32[1536,256]{1,0:T(8,128)}, f32[4,256,256]{2,1,0:T(8,128)S(1)}, f32[32,1024]{1,0:T(8,128)S(1)}) custom-call(f32[4608,128]{1,0:T(8,128)} %bitcast.2.packed_ref, f32[16,128]{1,0:T(8,128)S(1)} %bitcast.17, s32[8,128]{1,0:T(8,128)S(1)} %dynamic-slice_bitcast_fusion.3.rows_ref, f32[32,1024]{1,0:T(8,128)S(1)} %maximum_select_fusion.effects_ref, ...), custom_call_target="tpu_custom_call" | custom-call | tf_op jit(solution)/shard_map/factor/pallas_call | solution.py:576
  150.5 1.3 collective-permute-done.2.got_ref.there_ref
  151.8 2.4 %cross_share.1 = f32[32,512]{1,0:T(8,128)S(1)} custom-call(s32[1]{0:T(128)} %bitcast.core_ref, f32[32,1024]{1,0:T(8,128)S(1)} %get-tuple-element.28.shift_ref.here_ref, f32[32,1024]{1,0:T(8,128)S(1)} %collective-permute-done.2.got_ref.there_ref, f32[2,512,512]{2,1,0:T(8,128)} %cross.1.cross_ref), custom_call_target="tpu_custom_call" | custom-call | tf_op jit(solution)/shard_map/cross_share/pallas_call | solution.py:592
  154.2 1.0 collective-permute-start.3
  155.2 1.4 collective-permute-start.4
  156.6 2.2 %collective-permute-start.5 = (f32[32,512]{1,0:T(8,128)S(1)}, f32[32,512]{1,0:T(8,128)S(1)}, u32[]{:S(2)}, u32[]{:S(2)}) collective-permute-start(f32[32,512]{1,0:T(8,128)S(1)} %cross_share.1), channel_id=1, source_target_pairs={{0,6},{2,0},{4,2},{6,4},{8,14},{10,8},{12,10},{14,12},{16,22},{18,... | collective-permute-start | bytes 196616 | tf_op jit(solution)/shard_map/ppermute | solution.py:477
  158.7 4.5 %first_update.1 = (f32[32,3904]{1,0:T(8,128)S(1)}, f32[32,512]{1,0:T(8,128)S(1)}) custom-call(s32[1]{0:T(128)} %bitcast.core_ref, bf16[2,3904,512]{2,1,0:T(8,128)(2,1)} %own_ref.9, bf16[2,3904,512]{2,1,0:T(8,128)(2,1)} %collective-permute-done.other_ref, f32[32,1024]{1,0:T(8,128)S(1)} %get-tuple-element.28.shift_ref.here_ref, ...), custom_call_target="tpu_custom_call" | custom-call | flops 1023410176 | bytes 7995392 | tf_op jit(solution)/shard_map/first_update/pallas_call | solution.py:457
  163.3 0.9 collective-permute-start.8
  164.2 0.8 collective-permute-start.7
  165.0 2.4 %collective-permute-start.6 = (f32[32,512]{1,0:T(8,128)S(1)}, f32[32,512]{1,0:T(8,128)S(1)}, u32[]{:S(2)}, u32[]{:S(2)}) collective-permute-start(f32[32,512]{1,0:T(8,128)S(1)} %add_add_fusion.2), channel_id=1, source_target_pairs={{0,24},{2,26},{4,28},{6,30},{8,0},{10,2},{12,4},{14,6},{16,8},{18,... | collective-permute-start | bytes 196616 | tf_op jit(solution)/shard_map/ppermute | solution.py:477
  167.4 1.7 collective-permute-done.8
  169.2 0.7 collective-permute-done.7
  169.9 1.9 collective-permute-start.11
  171.9 3.1 %collective-permute-start.9 = (f32[32,512]{1,0:T(8,128)S(1)}, f32[32,512]{1,0:T(8,128)S(1)}, u32[]{:S(2)}, u32[]{:S(2)}) collective-permute-start(f32[32,512]{1,0:T(8,128)S(1)} %add_add_fusion.1), channel_id=1, source_target_pairs={{0,96},{2,98},{4,100},{6,102},{8,104},{10,106},{12,108},{14,110},{... | collective-permute-start | bytes 196616 | tf_op jit(solution)/shard_map/ppermute | solution.py:477
  175.0 0.7 collective-permute-done.11
  175.7 1.5 collective-permute-done.10
  177.3 1.2 collective-permute-done.12.got_ref
  178.6 7.2 %second.1.here_ref = f32[32,1152]{1,0:T(8,128)S(1)} custom-call(s32[1]{0:T(128)} %bitcast.core_ref, f32[32,1024]{1,0:T(8,128)S(1)} %get-tuple-element.28.shift_ref.here_ref, f32[32,512]{1,0:T(8,128)S(1)} %add_add_fusion.share_ref, f32[32,512]{1,0:T(8,128)S(1)} %collective-permute-done.12.got_ref, f32[1536,256]{1,0:T(8,128)} %get-tuple-element.34.panels_ref, ...), custom_call_target="tpu_custom_call" | custom-call | tf_op jit(solution)/shard_map/second/pallas_call | solution.py:613
  186.0 0.7 slice.4.norm_ref
  186.7 0.5 collective-permute-done.13.there_ref
  187.2 5.3 %last_update.1 = (f32[32,3904]{1,0:T(8,128)}, f32[2,32,512]{2,1,0:T(8,128)}, f32[1,32]{1,0:T(1,128)}) custom-call(s32[1]{0:T(128)} %bitcast.core_ref, bf16[2,3904,512]{2,1,0:T(8,128)(2,1)} %own_ref.9, bf16[2,3904,512]{2,1,0:T(8,128)(2,1)} %collective-permute-done.other_ref, f32[32,1152]{1,0:T(8,128)S(1)} %second.1.here_ref, ...), custom_call_target="tpu_custom_call" | custom-call | flops 1023410176 | bytes 7995392 | tf_op jit(solution)/shard_map/last_update/pallas_call | solution.py:457
  (38 shorter events, 1.0 us)
Async XLA Ops:
  0.6 78.8 %copy-start = (f32[2,32,1024]{2,1,0:T(8,128)S(1)}, f32[2,32,1024]{2,1,0:T(8,128)}, u32[]{:S(2)}) copy-start(f32[2,32,1024]{2,1,0:T(8,128)} %param.11) | copy-start | bytes 786436
  0.6 13.0 %collective-permute-start = (bf16[2,3904,512]{2,1,0:T(8,128)(2,1)}, bf16[2,3904,512]{2,1,0:T(8,128)(2,1)}, u32[]{:S(2)}, u32[]{:S(2)}) collective-permute-start(bf16[2,3904,512]{2,1,0:T(8,128)(2,1)} %own_ref.9), channel_id=1, source_target_pairs={{0,1},{1,0},{2,3},{3,2},{4,5},{5,4},{6,7},{7,6},{8,9},{9,8},{10,11... | collective-permute-start | bytes 23986184 | tf_op jit(solution)/shard_map/ppermute | solution.py:499
  0.7 1.0 copy-start.1
  23.4 11.9 %copy-start.3 = (f32[512,512]{1,0:T(8,128)S(1)}, f32[512,512]{1,0:T(8,128)}, u32[]{:S(2)}) copy-start(f32[512,512]{1,0:T(8,128)} %get-tuple-element.26.own_cross_ref) | copy-start | bytes 3145732
  23.4 44.4 %all-to-all-start = ((f32[64,72,128]{2,1,0:T(8,128)}), f32[64,72,128]{2,1,0:T(8,128)}, u32[]{:S(2)}, u32[]{:S(2)}) async-start(f32[64,72,128]{2,1,0:T(8,128)} %bitcast.19), calls=%async_computation | async-start | bytes 4718592 | tf_op jit(solution)/shard_map/all_to_all | solution.py:548
  71.0 7.9 %copy-start.4 = (f32[2,32,512]{2,1,0:T(8,128)S(1)}, f32[2,32,512]{2,1,0:T(8,128)}, u32[]{:S(2)}) copy-start(f32[2,32,512]{2,1,0:T(8,128)} %effects_ref.1) | copy-start | bytes 393220
  71.0 8.2 %copy-start.8 = (f32[32]{0:T(128)S(1)}, f32[32]{0:T(128)}, u32[]{:S(2)}) copy-start(f32[32]{0:T(128)} %param.14) | copy-start | bytes 388
  71.0 8.2 %copy-start.7 = (s32[2048]{0:T(1024)S(1)}, s32[2048]{0:T(1024)}, u32[]{:S(2)}) copy-start(s32[2048]{0:T(1024)} %param.13) | copy-start | bytes 24580
  71.0 40.1 %copy-start.5 = (f32[2048]{0:T(1024)S(1)}, f32[2048]{0:T(1024)}, u32[]{:S(2)}) copy-start(f32[2048]{0:T(1024)} %param.12) | copy-start | bytes 24580
  71.1 40.1 %all-to-all-start.1 = ((f32[64,72,128]{2,1,0:T(8,128)}), f32[64,72,128]{2,1,0:T(8,128)}, u32[]{:S(2)}, u32[]{:S(2)}) async-start(f32[64,72,128]{2,1,0:T(8,128)} %sums.1), calls=%async_computation.1 | async-start | bytes 4718592 | tf_op jit(solution)/shard_map/all_to_all | solution.py:564
  79.0 1.6 collective-permute-start.1
  111.2 47.5 %copy-start.2 = (f32[32,3904]{1,0:T(8,128)S(1)}, f32[32,3904]{1,0:T(8,128)}, u32[]{:S(2)}) copy-start(f32[32,3904]{1,0:T(8,128)} %residual_ref.5) | copy-start | bytes 1499140
  150.5 1.3 collective-permute-start.2
  154.2 9.0 %collective-permute-start.3 = (f32[32,512]{1,0:T(8,128)S(1)}, f32[32,512]{1,0:T(8,128)S(1)}, u32[]{:S(2)}, u32[]{:S(2)}) collective-permute-start(f32[32,512]{1,0:T(8,128)S(1)} %cross_share.1), channel_id=1, source_target_pairs={{0,2},{2,4},{4,6},{6,0},{8,10},{10,12},{12,14},{14,8},{16,18},{18,... | collective-permute-start | bytes 196616 | tf_op jit(solution)/shard_map/ppermute | solution.py:477
  155.2 8.1 %collective-permute-start.4 = (f32[32,512]{1,0:T(8,128)S(1)}, f32[32,512]{1,0:T(8,128)S(1)}, u32[]{:S(2)}, u32[]{:S(2)}) collective-permute-start(f32[32,512]{1,0:T(8,128)S(1)} %cross_share.1), channel_id=1, source_target_pairs={{0,4},{2,6},{4,0},{6,2},{8,12},{10,14},{12,8},{14,10},{16,20},{18,... | collective-permute-start | bytes 196616 | tf_op jit(solution)/shard_map/ppermute | solution.py:477
  156.6 6.7 %collective-permute-start.5 = (f32[32,512]{1,0:T(8,128)S(1)}, f32[32,512]{1,0:T(8,128)S(1)}, u32[]{:S(2)}, u32[]{:S(2)}) collective-permute-start(f32[32,512]{1,0:T(8,128)S(1)} %cross_share.1), channel_id=1, source_target_pairs={{0,6},{2,0},{4,2},{6,4},{8,14},{10,8},{12,10},{14,12},{16,22},{18,... | collective-permute-start | bytes 196616 | tf_op jit(solution)/shard_map/ppermute | solution.py:477
  163.3 5.9 %collective-permute-start.8 = (f32[32,512]{1,0:T(8,128)S(1)}, f32[32,512]{1,0:T(8,128)S(1)}, u32[]{:S(2)}, u32[]{:S(2)}) collective-permute-start(f32[32,512]{1,0:T(8,128)S(1)} %add_add_fusion.2), channel_id=1, source_target_pairs={{0,16},{2,18},{4,20},{6,22},{8,24},{10,26},{12,28},{14,30},{16,0},... | collective-permute-start | bytes 196616 | tf_op jit(solution)/shard_map/ppermute | solution.py:477
  164.2 5.7 %collective-permute-start.7 = (f32[32,512]{1,0:T(8,128)S(1)}, f32[32,512]{1,0:T(8,128)S(1)}, u32[]{:S(2)}, u32[]{:S(2)}) collective-permute-start(f32[32,512]{1,0:T(8,128)S(1)} %add_add_fusion.2), channel_id=1, source_target_pairs={{0,8},{2,10},{4,12},{6,14},{8,16},{10,18},{12,20},{14,22},{16,24},... | collective-permute-start | bytes 196616 | tf_op jit(solution)/shard_map/ppermute | solution.py:477
  165.0 4.9 %collective-permute-start.6 = (f32[32,512]{1,0:T(8,128)S(1)}, f32[32,512]{1,0:T(8,128)S(1)}, u32[]{:S(2)}, u32[]{:S(2)}) collective-permute-start(f32[32,512]{1,0:T(8,128)S(1)} %add_add_fusion.2), channel_id=1, source_target_pairs={{0,24},{2,26},{4,28},{6,30},{8,0},{10,2},{12,4},{14,6},{16,8},{18,... | collective-permute-start | bytes 196616 | tf_op jit(solution)/shard_map/ppermute | solution.py:477
  169.9 5.8 %collective-permute-start.11 = (f32[32,512]{1,0:T(8,128)S(1)}, f32[32,512]{1,0:T(8,128)S(1)}, u32[]{:S(2)}, u32[]{:S(2)}) collective-permute-start(f32[32,512]{1,0:T(8,128)S(1)} %add_add_fusion.1), channel_id=1, source_target_pairs={{0,64},{2,66},{4,68},{6,70},{8,72},{10,74},{12,76},{14,78},{16,80}... | collective-permute-start | bytes 196616 | tf_op jit(solution)/shard_map/ppermute | solution.py:477
  171.7 5.5 %collective-permute-start.10 = (f32[32,512]{1,0:T(8,128)S(1)}, f32[32,512]{1,0:T(8,128)S(1)}, u32[]{:S(2)}, u32[]{:S(2)}) collective-permute-start(f32[32,512]{1,0:T(8,128)S(1)} %add_add_fusion.1), channel_id=1, source_target_pairs={{0,32},{2,34},{4,36},{6,38},{8,40},{10,42},{12,44},{14,46},{16,48}... | collective-permute-start | bytes 196616 | tf_op jit(solution)/shard_map/ppermute | solution.py:477
  171.9 5.3 %collective-permute-start.9 = (f32[32,512]{1,0:T(8,128)S(1)}, f32[32,512]{1,0:T(8,128)S(1)}, u32[]{:S(2)}, u32[]{:S(2)}) collective-permute-start(f32[32,512]{1,0:T(8,128)S(1)} %add_add_fusion.1), channel_id=1, source_target_pairs={{0,96},{2,98},{4,100},{6,102},{8,104},{10,106},{12,108},{14,110},{... | collective-permute-start | bytes 196616 | tf_op jit(solution)/shard_map/ppermute | solution.py:477
  177.2 1.3 collective-permute-start.12
  178.6 8.6 %copy-start.6 = (f32[32]{0:T(128)S(1)}, f32[32]{0:T(128)}, u32[]{:S(2)}) copy-start(f32[32]{0:T(128)} %param.15) | copy-start | bytes 388
  185.8 1.4 collective-permute-start.13

commit v2 on v1

--- a/solution.py
+++ b/solution.py
@@ -66,17 +66,19 @@
     lane = lax.broadcasted_iota(jnp.int32, (SUB, TILE), 1)
     left = [tile[SUB * r : SUB * r + SUB, :] for r in range(groups)]
     done = []
+    pivot_cols = [spread(left[0][:, j : j + 1]) + zero for j in range(SUB)]
     for g in range(groups):
-        first = g * SUB
-        inside = (lane >= first) & (lane < first + SUB)
-        pivot_cols = [spread(left[g][:, first + j : first + j + 1]) + zero for j in range(SUB)]
-        cols = [[spread(left[r][:, first + j : first + j + 1]) for r in range(g + 1, groups)] for j in range(SUB)]
+        first, after = g * SUB, (g + 1) * SUB
+        last = g + 1 == groups
+        inside = (lane >= first) & (lane < after)
+        near = [] if last else [spread(left[g + 1][:, first + j : first + j + 1]) for j in range(SUB)]
+        coming = [] if last else [spread(left[g + 1][:, after + j : after + j + 1]) + zero for j in range(SUB)]
+        cols = [[spread(left[r][:, first + j : first + j + 1]) for r in range(g + 2, groups)] for j in range(SUB)]
         square = {(i, j): spread(pivot_cols[j][i : i + 1, :]) for j in range(SUB) for i in range(j + 1)}
         own = jnp.where(inside, jnp.where(lane == sub + first, 1.0, 0.0), left[g])
         rows = [spread(own[j : j + 1, :]) for j in range(SUB)]
-        last = g + 1 == groups
-        near = None if last else [cols[j][0] for j in range(SUB)]
         near_terms = []
+        near_solved = []
         share = {}
         solved = [None] * SUB
         pivots = jnp.zeros((SUB, TILE), F32)
@@ -102,22 +104,29 @@
                     near[k] = near[k] - (near[j] * one + near[j + 1] * two)
             solved[j], solved[j + 1] = rows[j] * ip + rows[j + 1] * iq, rows[j] * iq + rows[j + 1] * ir
             if not last:
+                near_solved += [near[j] * ip + near[j + 1] * iq, near[j] * iq + near[j + 1] * ir]
                 near_terms.append(near[j] * solved[j] + near[j + 1] * solved[j + 1])
         if not last:
+            pivot_cols = [
+                coming[j] - tree_sum([near[k] * spread(near_solved[k][j : j + 1, :]) for k in range(SUB)])
+                for j in range(SUB)
+            ]
             left[g + 1] = jnp.where(inside, 0.0, left[g + 1]) - tree_sum(near_terms)
         for j in (4, 5, 2, 3, 0, 1):
             solved[j] = solved[j] - tree_sum([share[j, k] * solved[k] for k in range(j // 2 * 2 + 2, SUB)])
         for r in range(g + 2, groups):
-            left[r] = jnp.where(inside, 0.0, left[r]) - tree_sum([cols[j][r - g - 1] * solved[j] for j in range(SUB)])
+            left[r] = jnp.where(inside, 0.0, left[r]) - tree_sum([cols[j][r - g - 2] * solved[j] for j in range(SUB)])
         root = lax.rsqrt(pivots)
         root = root * (1.5 - 0.5 * pivots * root * root)
-        done.append(jnp.where(lane < first + SUB, finished * root, 0.0))
+        done.append(jnp.where(lane < after, finished * root, 0.0))
     return jnp.concatenate(done, axis=0)
 
 
 def split_scores(residual, x):
+    chains = residual.shape[0]
     high, middle, _ = pieces_of(residual)
-    return dot_bf16(high, x, NN) + dot_bf16(middle, x, NN)
+    both = dot_bf16(jnp.concatenate([high, middle], axis=0), x, NN)
+    return both[:chains] + both[chains:]
 
 
 def chunk_loop(rows, body):
@@ -132,7 +141,6 @@
 
 
 def start_copies(sources, places, sems, rows):
-    copies = []
     for i, lo in enumerate(range(0, rows, CHUNK)):
         at = pl.ds(lo, min(CHUNK, rows - lo))
         for k, (source, place) in enumerate(zip(sources, places)):
@@ -232,17 +240,17 @@
     count, chains = layout.count, layout.chains
     put_diagonal(packed_ref, layout, core, square_ref)
     put_diagonal(packed_ref, layout, 1 - core, total.at[:, half:])
-    for r in range(count // 2):
-        for c in range(count // 2):
-            at = layout.lower(count // 2 + r, c)
-
-            @pl.when(core == 0)
-            def _():
-                packed_ref[at : at + TILE, :] = total[r * TILE : r * TILE + TILE, c * TILE : c * TILE + TILE]
-
-            @pl.when(core == 1)
-            def _():
-                packed_ref[at : at + TILE, :] = total[c * TILE : c * TILE + TILE, r * TILE : r * TILE + TILE].T
+    below = [(r, c, layout.lower(count // 2 + r, c)) for r in range(count // 2) for c in range(count // 2)]
+
+    @pl.when(core == 0)
+    def _():
+        for r, c, at in below:
+            packed_ref[at : at + TILE, :] = total[r * TILE : r * TILE + TILE, c * TILE : c * TILE + TILE]
+
+    @pl.when(core == 1)
+    def _():
+        for r, c, at in below:
+            packed_ref[at : at + TILE, :] = total[c * TILE : c * TILE + TILE, r * TILE : r * TILE + TILE].T
 
     for k, part in ((core, own_score_ref), (1 - core, score)):
         for col in range(count // 2):
@@ -309,11 +317,17 @@
 
 
 def factor_kernel(
-    layout, packed_ref, prior_ref, rows_ref, effects_ref, noise_ref, scale_ref, panels_ref, inverse_ref, shift_ref, factor_ref, zero_ref
+    layout, packed_hbm, prior_ref, rows_ref, effects_ref, noise_ref, scale_ref, panels_hbm, inverse_hbm, shift_ref,
+    packed_ref, panels_ref, inverse_ref, factor_ref, zero_ref, sems
 ):
     width = factor_ref.shape[1]
     count = width // TILE
     chains = effects_ref.shape[0]
+    halfway = layout.lower(count * 3 // 4, 0)
+    parts = [slice(0, halfway), slice(halfway, layout.pairs), slice(layout.pairs, layout.rows)]
+    arrivals = [pltpu.make_async_copy(packed_hbm.at[at], packed_ref.at[at], sems.at[i]) for i, at in enumerate(parts)]
+    for arrival in arrivals:
+        arrival.start()
     table_rows = rows_ref[...]
     high = lax.shift_right_logical(table_rows, 7)
     low = lax.bitwise_and(table_rows, TILE - 1)
@@ -325,9 +339,14 @@
     diagonal = lax.broadcasted_iota(jnp.int32, (TILE, TILE), 0) == lax.broadcasted_iota(jnp.int32, (TILE, TILE), 1)
     for row in range(count):
         rows = slice(row * TILE, row * TILE + TILE)
+        if row in (0, count * 3 // 4):
+            arrivals[0 if row == 0 else 1].wait()
         for col in range(row):
             at = layout.lower(row, col)
             factor_ref[rows, col * TILE : col * TILE + TILE] = packed_ref[at : at + TILE, :]
+    arrivals[2].wait()
+    for row in range(count):
+        rows = slice(row * TILE, row * TILE + TILE)
         triangle, middle = get_diagonal(packed_ref, layout, row)
         middle = middle + jnp.where(diagonal, inverse_prior[row : row + 1, :], 0.0)
         factor_ref[rows, rows] = triangle + triangle.T + middle
@@ -370,30 +389,54 @@
     ]
     for k in range(width // STRIP - 1):
         panels_ref[panel_rows(width, k), :] = factor_ref[(k + 1) * STRIP : width, k * STRIP : (k + 1) * STRIP]
+    departures = [
+        pltpu.make_async_copy(panels_ref, panels_hbm, sems.at[3]),
+        pltpu.make_async_copy(inverse_ref, inverse_hbm, sems.at[4]),
+    ]
+    for departure in departures:
+        departure.start()
     for j, part in enumerate(backward(moved, panels_ref, inverse_ref)):
         shift_ref[:, j * STRIP : j * STRIP + STRIP] = part
-
-
-def cross_share_kernel(core_ref, shift_ref, got_ref, cross_ref, share_ref):
+    for departure in departures:
+        departure.wait()
+
+
+def cross_share_kernel(core_ref, shift_ref, got_ref, cross_hbm, share_ref, cross_ref, sems):
     core = core_ref[0]
     half = cross_ref.shape[1]
+    arrivals = [pltpu.make_async_copy(cross_hbm.at[i], cross_ref.at[i], sems.at[i]) for i in range(2)]
+    for arrival in arrivals:
+        arrival.start()
     shift = jnp.where(core == 0, shift_ref[...], got_ref[...])
     change = shift.astype(BF16)
     first, last = change[:, :half], change[:, half:]
     mine = jnp.where(core == 0, first, last)
     theirs = jnp.where(core == 0, last, first)
-    share_ref[...] = sum(
-        dot_bf16(change, part, NN) for change, ref in ((mine, cross_ref[0]), (theirs, cross_ref[1])) for part in pieces_of(ref)
-    )
-
-
-def second_kernel(layout, core_ref, shift_ref, share_ref, got_ref, panels_ref, inverse_ref, packed_ref, final_ref):
+    total = None
+    for i, part in enumerate((mine, theirs)):
+        arrivals[i].wait()
+        product = sum(dot_bf16(part, piece, NN) for piece in pieces_of(cross_ref[i]))
+        total = product if total is None else total + product
+    share_ref[...] = total
+
+
+def second_kernel(
+    layout, core_ref, shift_ref, share_ref, got_ref, panels_hbm, inverse_hbm, packed_hbm, final_ref,
+    panels_ref, inverse_ref, packed_ref, sems
+):
     width, count, chains = shift_ref.shape[1], layout.count, layout.chains
+    pairs = ((inverse_hbm, inverse_ref), (panels_hbm, panels_ref), (packed_hbm, packed_ref))
+    arrivals = [pltpu.make_async_copy(source, place, sems.at[i]) for i, (source, place) in enumerate(pairs)]
+    for arrival in arrivals:
+        arrival.start()
     keep = jnp.where(core_ref[0] == 1, 1.0, 0.0)
     right = jnp.concatenate([got_ref[...], share_ref[...]], axis=1) * keep
     moved = [right[:, j : j + STRIP] for j in range(0, width, STRIP)]
+    arrivals[0].wait()
     for k in range(len(moved)):
         moved[k] = dot_rows(moved[k], inverse_ref[k], NT)
+        if k == 0:
+            arrivals[1].wait()
         lo = (k + 1) * STRIP
         if lo < width:
             change_by = dot_rows(moved[k], panels_ref[panel_rows(width, k), :], NT)
@@ -405,6 +448,7 @@
     change = final_ref[:, :width].astype(BF16)
     value = change.astype(F32)
     total = jnp.zeros((chains, TILE), F32)
+    arrivals[2].wait()
     for row in range(count):
         cols = slice(row * TILE, row * TILE + TILE)
         triangle, middle = get_diagonal(packed_ref, layout, row)
@@ -573,16 +617,25 @@
     block_noise = lax.dynamic_index_in_dim(noise, core, 0, keepdims=False)
     block_rows = lax.dynamic_index_in_dim(block_snps.reshape(blocks, count, TILE), core, 0, keepdims=False)
     scale = jnp.sqrt(noise_var)[:, None]
+    panels_shape = (panel_rows(width, width // STRIP - 1).start, STRIP)
+    inverse_shape = (width // STRIP, STRIP, STRIP)
     panels, inverse, shift = pl.pallas_call(
         functools.partial(factor_kernel, layout),
         out_shape=(
-            jax.ShapeDtypeStruct((panel_rows(width, width // STRIP - 1).start, STRIP), F32),
-            jax.ShapeDtypeStruct((width // STRIP, STRIP, STRIP), F32),
+            jax.ShapeDtypeStruct(panels_shape, F32),
+            jax.ShapeDtypeStruct(inverse_shape, F32),
             jax.ShapeDtypeStruct((chains, width), F32),
         ),
-        in_specs=[VMEM] * 6,
-        out_specs=(VMEM,) * 3,
-        scratch_shapes=[pltpu.VMEM((width + chains, width), F32), pltpu.VMEM((SUB, TILE), F32)],
+        in_specs=[ANY] + [VMEM] * 5,
+        out_specs=(ANY, ANY, VMEM),
+        scratch_shapes=[
+            pltpu.VMEM(packed.shape, F32),
+            pltpu.VMEM(panels_shape, F32),
+            pltpu.VMEM(inverse_shape, F32),
+            pltpu.VMEM((width + chains, width), F32),
+            pltpu.VMEM((SUB, TILE), F32),
+            pltpu.SemaphoreType.DMA((5,)),
+        ],
         compiler_params=PARAMS,
         cost_estimate=pl.CostEstimate(flops=0, bytes_accessed=0, transcendentals=0),
         name="factor",
@@ -592,8 +645,9 @@
     share = pl.pallas_call(
         cross_share_kernel,
         out_shape=jax.ShapeDtypeStruct((chains, half), F32),
-        in_specs=[SMEM] + [VMEM] * 3,
+        in_specs=[SMEM] + [VMEM] * 2 + [ANY],
         out_specs=VMEM,
+        scratch_shapes=[pltpu.VMEM(cross.shape, F32), pltpu.SemaphoreType.DMA((2,))],
         compiler_params=PARAMS,
         name="cross_share",
     )(core_arg, shift, got_shift, cross)
@@ -613,8 +667,14 @@
     final = pl.pallas_call(
         functools.partial(second_kernel, layout),
         out_shape=jax.ShapeDtypeStruct((chains, width + TILE), F32),
-        in_specs=[SMEM] + [VMEM] * 6,
+        in_specs=[SMEM] + [VMEM] * 3 + [ANY] * 3,
         out_specs=VMEM,
+        scratch_shapes=[
+            pltpu.VMEM(panels_shape, F32),
+            pltpu.VMEM(inverse_shape, F32),
+            pltpu.VMEM(packed.shape, F32),
+            pltpu.SemaphoreType.DMA((3,)),
+        ],
         compiler_params=PARAMS,
         name="second",
     )(core_arg, shift, share, got, panels, inverse, packed)

time: 194 us -> 187 us (0.964)
  Pallas kernels: 85.7 us -> 79.5 us
    pallas_call x1, Pallas kernels: 39.3 us -> 35.7 us  [local(): pl.pallas_call(functools.partial(factor_kernel, layout), out_shape=(jax.S...]
where the time goes in v2:
time: 187 us; the launch traced here: 185 us
  Pallas kernels  79.5 us (43%)
  waiting for transfers between devices  69.5 us (37%)
  starting transfers between devices  33 us (18%)
  local copies, waits for them, and re-layouts  1.93 us (1%)
    pallas_call x1, Pallas kernels, local(): pl.pallas_call(functools.partial(factor_kernel, layout), out_shape=(jax.S...  35.7 us
    all_to_all x1, waiting for transfers between devices, local(): packed = lax.all_to_all(packed, 'ind', 0, 0).reshape(spots * piece, TILE)  29.5 us
    all_to_all x1, waiting for transfers between devices, local(): packed = lax.all_to_all(packed.reshape(spots, piece, TILE), 'ind', 0, 0)  26.9 us
    ppermute x9, starting transfers between devices, line_sums(): lax.ppermute(value, 'ind', [(i, i + ((at[i] + step) % LINE - at[i]) * str...  13.3 us
    all_to_all x1, starting transfers between devices, local(): packed = lax.all_to_all(packed.reshape(spots, piece, TILE), 'ind', 0, 0)  11.9 us
    pallas_call x2, Pallas kernels, update_call(): pl.pallas_call(kernel, out_shape=out_shape, in_specs=[SMEM, ANY, ANY] + [...  9.81 us
    pallas_call x1, Pallas kernels, local(): pl.pallas_call(functools.partial(gram_kernel, layout), out_shape=jax.Shap...  8.92 us
    pallas_call x1, Pallas kernels, local(): pl.pallas_call(own_kernel, out_shape=(jax.ShapeDtypeStruct((half, half),...  7.57 us
  transfers between devices with their start and end apart: 16, of which 11 were waited for; matrix products, arithmetic and copies ran while one was open for 0% of the time, Pallas kernels for 10%

profile of v2, /device:TPU:0, one launch (start us, length us, event | category | flops | bytes accessed | tf_op | source)
XLA Modules:
  0.0 185.1 jit_solution(2906166283352345577)
XLA Ops:
  0.8 1.0 copy-done.1
  1.8 7.6 %own.1 = (f32[512,512]{1,0:T(8,128)S(1)}, f32[32,512]{1,0:T(8,128)S(1)}, f32[512,512]{1,0:T(8,128)}) custom-call(s32[1]{0:T(128)} %bitcast.core_ref, bf16[2,3904,512]{2,1,0:T(8,128)(2,1)} %own_ref.9, f32[32,3904]{1,0:T(8,128)S(1)} %copy-done.1), custom_call_target="tpu_custom_call" | custom-call | flops 2046820352 | bytes 3997696 | tf_op jit(solution)/shard_map/own/pallas_call | solution.py:548
  9.4 4.3 %collective-permute-done.other_ref = bf16[2,3904,512]{2,1,0:T(8,128)(2,1)} collective-permute-done((bf16[2,3904,512]{2,1,0:T(8,128)(2,1)}, bf16[2,3904,512]{2,1,0:T(8,128)(2,1)}, u32[]{:S(2)}, u32[]{:S(2)}) %collective-permute-start) | collective-permute-done | bytes 7995424 | tf_op jit(solution)/shard_map/ppermute | solution.py:543
  13.7 8.9 %gram.1 = f32[4608,128]{1,0:T(8,128)} custom-call(s32[1]{0:T(128)} %bitcast.core_ref, bf16[2,3904,512]{2,1,0:T(8,128)(2,1)} %own_ref.9, bf16[2,3904,512]{2,1,0:T(8,128)(2,1)} %collective-permute-done.other_ref, f32[32,3904]{1,0:T(8,128)S(1)} %copy-done.1, f32[512,512]{1,0:T(8,128)S(1)} %get-tuple-element.22.square_ref, ...), custom_call_target="tpu_custom_call" | custom-call | tf_op jit(solution)/shard_map/gram/pallas_call | solution.py:562
  22.6 11.9 %all-to-all-start = ((f32[64,72,128]{2,1,0:T(8,128)}), f32[64,72,128]{2,1,0:T(8,128)}, u32[]{:S(2)}, u32[]{:S(2)}) async-start(f32[64,72,128]{2,1,0:T(8,128)} %bitcast.19), calls=%async_computation | async-start | bytes 4718592 | tf_op jit(solution)/shard_map/all_to_all | solution.py:592
  34.5 5.9 %cross.1.cross_hbm = f32[2,512,512]{2,1,0:T(8,128)} custom-call(bf16[2,3904,512]{2,1,0:T(8,128)(2,1)} %own_ref.9, bf16[2,3904,512]{2,1,0:T(8,128)(2,1)} %collective-permute-done.other_ref, f32[512,512]{1,0:T(8,128)S(1)} %copy-done.3), custom_call_target="tpu_custom_call" | custom-call | flops 2046820352 | bytes 7995392 | tf_op jit(solution)/shard_map/cross/pallas_call | solution.py:579
  40.4 26.9 %all-to-all-done.parts_ref = f32[64,72,128]{2,1,0:T(8,128)} async-done(((f32[64,72,128]{2,1,0:T(8,128)}), f32[64,72,128]{2,1,0:T(8,128)}, u32[]{:S(2)}, u32[]{:S(2)}) %all-to-all-start) | async-done | bytes 2359328 | tf_op jit(solution)/shard_map/all_to_all | solution.py:592
  67.3 3.2 %sums.1 = f32[64,72,128]{2,1,0:T(8,128)} custom-call(f32[64,72,128]{2,1,0:T(8,128)} %all-to-all-done.parts_ref), custom_call_target="tpu_custom_call" | custom-call | tf_op jit(solution)/shard_map/sums/pallas_call | solution.py:594
  70.5 6.8 %all-to-all-start.1 = ((f32[64,72,128]{2,1,0:T(8,128)}), f32[64,72,128]{2,1,0:T(8,128)}, u32[]{:S(2)}, u32[]{:S(2)}) async-start(f32[64,72,128]{2,1,0:T(8,128)} %sums.1), calls=%async_computation.1 | async-start | bytes 4718592 | tf_op jit(solution)/shard_map/all_to_all | solution.py:608
  77.8 1.2 collective-permute-done.1
  79.0 29.5 %all-to-all-done.1 = f32[64,72,128]{2,1,0:T(8,128)} async-done(((f32[64,72,128]{2,1,0:T(8,128)}), f32[64,72,128]{2,1,0:T(8,128)}, u32[]{:S(2)}, u32[]{:S(2)}) %all-to-all-start.1) | async-done | bytes 2359328 | tf_op jit(solution)/shard_map/all_to_all | solution.py:608
  108.5 35.7 %factor.1 = (f32[1536,256]{1,0:T(8,128)}, f32[4,256,256]{2,1,0:T(8,128)S(1)}, f32[32,1024]{1,0:T(8,128)S(1)}) custom-call(f32[4608,128]{1,0:T(8,128)} %bitcast.2.packed_hbm, f32[16,128]{1,0:T(8,128)S(1)} %bitcast.17, s32[8,128]{1,0:T(8,128)S(1)} %dynamic-slice_bitcast_fusion.3.rows_ref, f32[32,1024]{1,0:T(8,128)S(1)} %maximum_select_fusion.effects_ref, ...), custom_call_target="tpu_custom_call" | custom-call | tf_op jit(solution)/shard_map/factor/pallas_call | solution.py:622
  144.6 1.3 collective-permute-done.2.got_ref.there_ref
  145.9 2.0 %cross_share.1 = f32[32,512]{1,0:T(8,128)S(1)} custom-call(s32[1]{0:T(128)} %bitcast.core_ref, f32[32,1024]{1,0:T(8,128)S(1)} %get-tuple-element.28.shift_ref.here_ref, f32[32,1024]{1,0:T(8,128)S(1)} %collective-permute-done.2.got_ref.there_ref, f32[2,512,512]{2,1,0:T(8,128)} %cross.1.cross_hbm), custom_call_target="tpu_custom_call" | custom-call | tf_op jit(solution)/shard_map/cross_share/pallas_call | solution.py:645
  148.0 1.0 collective-permute-start.3
  149.0 1.4 collective-permute-start.4
  150.3 2.2 %collective-permute-start.5 = (f32[32,512]{1,0:T(8,128)S(1)}, f32[32,512]{1,0:T(8,128)S(1)}, u32[]{:S(2)}, u32[]{:S(2)}) collective-permute-start(f32[32,512]{1,0:T(8,128)S(1)} %cross_share.1), channel_id=1, source_target_pairs={{0,6},{2,0},{4,2},{6,4},{8,14},{10,8},{12,10},{14,12},{16,22},{18,... | collective-permute-start | bytes 196616 | tf_op jit(solution)/shard_map/ppermute | solution.py:521
  152.5 4.5 %first_update.1 = (f32[32,3904]{1,0:T(8,128)S(1)}, f32[32,512]{1,0:T(8,128)S(1)}) custom-call(s32[1]{0:T(128)} %bitcast.core_ref, bf16[2,3904,512]{2,1,0:T(8,128)(2,1)} %own_ref.9, bf16[2,3904,512]{2,1,0:T(8,128)(2,1)} %collective-permute-done.other_ref, f32[32,1024]{1,0:T(8,128)S(1)} %get-tuple-element.28.shift_ref.here_ref, ...), custom_call_target="tpu_custom_call" | custom-call | flops 1023410176 | bytes 7995392 | tf_op jit(solution)/shard_map/first_update/pallas_call | solution.py:501
  157.1 1.0 collective-permute-start.8
  158.1 0.6 collective-permute-start.7
  158.7 2.6 %collective-permute-start.6 = (f32[32,512]{1,0:T(8,128)S(1)}, f32[32,512]{1,0:T(8,128)S(1)}, u32[]{:S(2)}, u32[]{:S(2)}) collective-permute-start(f32[32,512]{1,0:T(8,128)S(1)} %add_add_fusion.2), channel_id=1, source_target_pairs={{0,24},{2,26},{4,28},{6,30},{8,0},{10,2},{12,4},{14,6},{16,8},{18,... | collective-permute-start | bytes 196616 | tf_op jit(solution)/shard_map/ppermute | solution.py:521
  161.3 1.6 collective-permute-done.8
  162.9 0.7 collective-permute-done.7
  163.7 1.3 collective-permute-start.11
  164.9 0.7 collective-permute-start.10
  165.7 2.5 %collective-permute-start.9 = (f32[32,512]{1,0:T(8,128)S(1)}, f32[32,512]{1,0:T(8,128)S(1)}, u32[]{:S(2)}, u32[]{:S(2)}) collective-permute-start(f32[32,512]{1,0:T(8,128)S(1)} %add_add_fusion.1), channel_id=1, source_target_pairs={{0,96},{2,98},{4,100},{6,102},{8,104},{10,106},{12,108},{14,110},{... | collective-permute-start | bytes 196616 | tf_op jit(solution)/shard_map/ppermute | solution.py:521
  168.2 1.3 collective-permute-done.11
  169.5 0.9 collective-permute-done.10
  170.5 1.2 collective-permute-done.12.got_ref
  171.8 6.4 %second.1.here_ref = f32[32,1152]{1,0:T(8,128)S(1)} custom-call(s32[1]{0:T(128)} %bitcast.core_ref, f32[32,1024]{1,0:T(8,128)S(1)} %get-tuple-element.28.shift_ref.here_ref, f32[32,512]{1,0:T(8,128)S(1)} %add_add_fusion.share_ref, f32[32,512]{1,0:T(8,128)S(1)} %collective-permute-done.12.got_ref, f32[1536,256]{1,0:T(8,128)} %get-tuple-element.34.panels_hbm, ...), custom_call_target="tpu_custom_call" | custom-call | tf_op jit(solution)/shard_map/second/pallas_call | solution.py:667
  178.4 0.7 slice.4.norm_ref
  179.6 5.3 %last_update.1 = (f32[32,3904]{1,0:T(8,128)}, f32[2,32,512]{2,1,0:T(8,128)}, f32[1,32]{1,0:T(1,128)}) custom-call(s32[1]{0:T(128)} %bitcast.core_ref, bf16[2,3904,512]{2,1,0:T(8,128)(2,1)} %own_ref.9, bf16[2,3904,512]{2,1,0:T(8,128)(2,1)} %collective-permute-done.other_ref, f32[32,1152]{1,0:T(8,128)S(1)} %second.1.here_ref, ...), custom_call_target="tpu_custom_call" | custom-call | flops 1023410176 | bytes 7995392 | tf_op jit(solution)/shard_map/last_update/pallas_call | solution.py:501
  (38 shorter events, 1.7 us)
Async XLA Ops:
  0.6 77.2 %copy-start = (f32[2,32,1024]{2,1,0:T(8,128)S(1)}, f32[2,32,1024]{2,1,0:T(8,128)}, u32[]{:S(2)}) copy-start(f32[2,32,1024]{2,1,0:T(8,128)} %param.11) | copy-start | bytes 786436
  0.6 13.0 %collective-permute-start = (bf16[2,3904,512]{2,1,0:T(8,128)(2,1)}, bf16[2,3904,512]{2,1,0:T(8,128)(2,1)}, u32[]{:S(2)}, u32[]{:S(2)}) collective-permute-start(bf16[2,3904,512]{2,1,0:T(8,128)(2,1)} %own_ref.9), channel_id=1, source_target_pairs={{0,1},{1,0},{2,3},{3,2},{4,5},{5,4},{6,7},{7,6},{8,9},{9,8},{10,11... | collective-permute-start | bytes 23986184 | tf_op jit(solution)/shard_map/ppermute | solution.py:543
  0.7 1.0 copy-start.1
  22.6 11.9 %copy-start.3 = (f32[512,512]{1,0:T(8,128)S(1)}, f32[512,512]{1,0:T(8,128)}, u32[]{:S(2)}) copy-start(f32[512,512]{1,0:T(8,128)} %get-tuple-element.26.own_cross_ref) | copy-start | bytes 3145732
  22.6 44.7 %all-to-all-start = ((f32[64,72,128]{2,1,0:T(8,128)}), f32[64,72,128]{2,1,0:T(8,128)}, u32[]{:S(2)}, u32[]{:S(2)}) async-start(f32[64,72,128]{2,1,0:T(8,128)} %bitcast.19), calls=%async_computation | async-start | bytes 4718592 | tf_op jit(solution)/shard_map/all_to_all | solution.py:592
  70.5 6.9 %copy-start.4 = (f32[2,32,512]{2,1,0:T(8,128)S(1)}, f32[2,32,512]{2,1,0:T(8,128)}, u32[]{:S(2)}) copy-start(f32[2,32,512]{2,1,0:T(8,128)} %effects_ref.1) | copy-start | bytes 393220
  70.5 7.2 %copy-start.8 = (f32[32]{0:T(128)S(1)}, f32[32]{0:T(128)}, u32[]{:S(2)}) copy-start(f32[32]{0:T(128)} %param.14) | copy-start | bytes 388
  70.5 7.2 %copy-start.7 = (s32[2048]{0:T(1024)S(1)}, s32[2048]{0:T(1024)}, u32[]{:S(2)}) copy-start(s32[2048]{0:T(1024)} %param.13) | copy-start | bytes 24580
  70.5 38.0 %copy-start.5 = (f32[2048]{0:T(1024)S(1)}, f32[2048]{0:T(1024)}, u32[]{:S(2)}) copy-start(f32[2048]{0:T(1024)} %param.12) | copy-start | bytes 24580
  70.5 38.0 %all-to-all-start.1 = ((f32[64,72,128]{2,1,0:T(8,128)}), f32[64,72,128]{2,1,0:T(8,128)}, u32[]{:S(2)}, u32[]{:S(2)}) async-start(f32[64,72,128]{2,1,0:T(8,128)} %sums.1), calls=%async_computation.1 | async-start | bytes 4718592 | tf_op jit(solution)/shard_map/all_to_all | solution.py:608
  77.3 1.6 collective-permute-start.1
  108.5 44.0 %copy-start.2 = (f32[32,3904]{1,0:T(8,128)S(1)}, f32[32,3904]{1,0:T(8,128)}, u32[]{:S(2)}) copy-start(f32[32,3904]{1,0:T(8,128)} %residual_ref.5) | copy-start | bytes 1499140
  144.3 1.6 collective-permute-start.2
  148.0 9.1 %collective-permute-start.3 = (f32[32,512]{1,0:T(8,128)S(1)}, f32[32,512]{1,0:T(8,128)S(1)}, u32[]{:S(2)}, u32[]{:S(2)}) collective-permute-start(f32[32,512]{1,0:T(8,128)S(1)} %cross_share.1), channel_id=1, source_target_pairs={{0,2},{2,4},{4,6},{6,0},{8,10},{10,12},{12,14},{14,8},{16,18},{18,... | collective-permute-start | bytes 196616 | tf_op jit(solution)/shard_map/ppermute | solution.py:521
  149.0 8.0 %collective-permute-start.4 = (f32[32,512]{1,0:T(8,128)S(1)}, f32[32,512]{1,0:T(8,128)S(1)}, u32[]{:S(2)}, u32[]{:S(2)}) collective-permute-start(f32[32,512]{1,0:T(8,128)S(1)} %cross_share.1), channel_id=1, source_target_pairs={{0,4},{2,6},{4,0},{6,2},{8,12},{10,14},{12,8},{14,10},{16,20},{18,... | collective-permute-start | bytes 196616 | tf_op jit(solution)/shard_map/ppermute | solution.py:521
  150.3 6.7 %collective-permute-start.5 = (f32[32,512]{1,0:T(8,128)S(1)}, f32[32,512]{1,0:T(8,128)S(1)}, u32[]{:S(2)}, u32[]{:S(2)}) collective-permute-start(f32[32,512]{1,0:T(8,128)S(1)} %cross_share.1), channel_id=1, source_target_pairs={{0,6},{2,0},{4,2},{6,4},{8,14},{10,8},{12,10},{14,12},{16,22},{18,... | collective-permute-start | bytes 196616 | tf_op jit(solution)/shard_map/ppermute | solution.py:521
  157.1 5.9 %collective-permute-start.8 = (f32[32,512]{1,0:T(8,128)S(1)}, f32[32,512]{1,0:T(8,128)S(1)}, u32[]{:S(2)}, u32[]{:S(2)}) collective-permute-start(f32[32,512]{1,0:T(8,128)S(1)} %add_add_fusion.2), channel_id=1, source_target_pairs={{0,16},{2,18},{4,20},{6,22},{8,24},{10,26},{12,28},{14,30},{16,0},... | collective-permute-start | bytes 196616 | tf_op jit(solution)/shard_map/ppermute | solution.py:521
  158.1 5.5 %collective-permute-start.7 = (f32[32,512]{1,0:T(8,128)S(1)}, f32[32,512]{1,0:T(8,128)S(1)}, u32[]{:S(2)}, u32[]{:S(2)}) collective-permute-start(f32[32,512]{1,0:T(8,128)S(1)} %add_add_fusion.2), channel_id=1, source_target_pairs={{0,8},{2,10},{4,12},{6,14},{8,16},{10,18},{12,20},{14,22},{16,24},... | collective-permute-start | bytes 196616 | tf_op jit(solution)/shard_map/ppermute | solution.py:521
  158.7 4.9 %collective-permute-start.6 = (f32[32,512]{1,0:T(8,128)S(1)}, f32[32,512]{1,0:T(8,128)S(1)}, u32[]{:S(2)}, u32[]{:S(2)}) collective-permute-start(f32[32,512]{1,0:T(8,128)S(1)} %add_add_fusion.2), channel_id=1, source_target_pairs={{0,24},{2,26},{4,28},{6,30},{8,0},{10,2},{12,4},{14,6},{16,8},{18,... | collective-permute-start | bytes 196616 | tf_op jit(solution)/shard_map/ppermute | solution.py:521
  163.7 5.8 %collective-permute-start.11 = (f32[32,512]{1,0:T(8,128)S(1)}, f32[32,512]{1,0:T(8,128)S(1)}, u32[]{:S(2)}, u32[]{:S(2)}) collective-permute-start(f32[32,512]{1,0:T(8,128)S(1)} %add_add_fusion.1), channel_id=1, source_target_pairs={{0,64},{2,66},{4,68},{6,70},{8,72},{10,74},{12,76},{14,78},{16,80}... | collective-permute-start | bytes 196616 | tf_op jit(solution)/shard_map/ppermute | solution.py:521
  164.9 5.5 %collective-permute-start.10 = (f32[32,512]{1,0:T(8,128)S(1)}, f32[32,512]{1,0:T(8,128)S(1)}, u32[]{:S(2)}, u32[]{:S(2)}) collective-permute-start(f32[32,512]{1,0:T(8,128)S(1)} %add_add_fusion.1), channel_id=1, source_target_pairs={{0,32},{2,34},{4,36},{6,38},{8,40},{10,42},{12,44},{14,46},{16,48}... | collective-permute-start | bytes 196616 | tf_op jit(solution)/shard_map/ppermute | solution.py:521
  165.7 4.8 %collective-permute-start.9 = (f32[32,512]{1,0:T(8,128)S(1)}, f32[32,512]{1,0:T(8,128)S(1)}, u32[]{:S(2)}, u32[]{:S(2)}) collective-permute-start(f32[32,512]{1,0:T(8,128)S(1)} %add_add_fusion.1), channel_id=1, source_target_pairs={{0,96},{2,98},{4,100},{6,102},{8,104},{10,106},{12,108},{14,110},{... | collective-permute-start | bytes 196616 | tf_op jit(solution)/shard_map/ppermute | solution.py:521
  170.4 1.3 collective-permute-start.12
  171.8 7.9 %copy-start.6 = (f32[32]{0:T(128)S(1)}, f32[32]{0:T(128)}, u32[]{:S(2)}) copy-start(f32[32]{0:T(128)} %param.15) | copy-start | bytes 388
  178.2 1.5 collective-permute-start.13

commit v3 on v2

--- a/solution.py
+++ b/solution.py
@@ -52,6 +52,16 @@
     two = dot_bf16(jnp.concatenate(parts[:2], axis=0), middle, dims)
     three = dot_bf16(parts[0], low, dims)
     return one[:rows] + ((one[rows : 2 * rows] + two[:rows]) + (one[2 * rows :] + two[rows:] + three))
+
+
+def dot_narrow(left, right):
+    high, middle, low = pieces_of(left)
+    right_high, right_middle, right_low = pieces_of(right)
+    columns = right.shape[0]
+    both = jnp.concatenate([jnp.concatenate([part, part], axis=1) for part in (right_high, right_middle)], axis=0)
+    one = dot_bf16(jnp.concatenate([high, middle], axis=1), both, NT)
+    two = dot_bf16(jnp.concatenate([high, low], axis=1), jnp.concatenate([right_low, right_high], axis=1), NT)
+    return one[:, :columns] + (one[:, columns:] + two)
 
 
 def tree_sum(terms):
@@ -368,10 +378,10 @@
                 lo, hi = step * TILE, (step + 1) * TILE
                 side = slice(step % 2 * TILE, step % 2 * TILE + TILE)
                 inverse = inverse_ref[step // 2, side, side]
-                factor_ref[hi:, lo:hi] = dot_exact(factor_ref[hi:, lo:hi], inverse, NT)
+                factor_ref[hi:, lo:hi] = dot_narrow(factor_ref[hi:, lo:hi], inverse)
                 if step % 2 == 0:
                     panel = factor_ref[hi:, lo:hi]
-                    factor_ref[hi:, hi : hi + TILE] = factor_ref[hi:, hi : hi + TILE] - dot_exact(panel, panel[:TILE, :], NT)
+                    factor_ref[hi:, hi : hi + TILE] = factor_ref[hi:, hi : hi + TILE] - dot_narrow(panel, panel[:TILE, :])
                 else:
                     for c in range(hi, width, STRIP):
                         panel = factor_ref[c:, lo - TILE : hi]
@@ -461,43 +471,71 @@
     final_ref[:, width:] = jnp.broadcast_to(jnp.sum(total, axis=1, keepdims=True), (chains, TILE))
 
 
-def update_rows(block, core, own_ref, other_ref, shift, residual_ref, new_ref, x, sems):
-    rows, half = own_ref.shape[1:]
-    sources, places = [own_ref.at[block], other_ref.at[block]], [x.at[0], x.at[1]]
-    start_copies(sources, places, sems, rows)
-    mine = jnp.where(core == 0, shift[:, :half], shift[:, half:])
-    theirs = jnp.where(core == 0, shift[:, half:], shift[:, :half])
-    own_change, their_change = mine.astype(BF16), theirs.astype(BF16)
-    for i, start in enumerate(range(0, rows, CHUNK)):
-        size = min(CHUNK, rows - start)
-        wait_copies(sources, places, sems, i, start, size)
-        at = pl.ds(start, size)
-        change = dot_bf16(own_change, x[0, at, :], NT) + dot_bf16(their_change, x[1, at, :], NT)
-        new_ref[:, at] = residual_ref[:, at] - change
-    return mine
-
-
-def first_update_kernel(core_ref, own_ref, other_ref, here_ref, there_ref, residual_ref, new_ref, mine_ref, x, sems):
+def halves(shift, core):
+    half = shift.shape[1] // 2
+    first, last = shift[:, :half], shift[:, half:]
+    return jnp.where(core == 0, first, last), jnp.where(core == 0, last, first)
+
+
+def update_rows(block, rows, own_ref, other_ref, changes, get, put, x, sems):
+    chunks = [(lo, min(lo + CHUNK, rows[1])) for lo in range(rows[0], rows[1], CHUNK)]
+    copies = []
+    for i, (lo, hi) in enumerate(chunks):
+        pair = [
+            pltpu.make_async_copy(
+                source.at[block, lo:hi, :], x.at[k, lo - rows[0] : hi - rows[0], :], sems.at[i, k]
+            )
+            for k, source in enumerate((own_ref, other_ref))
+        ]
+        for copy in pair:
+            copy.start()
+        copies.append(pair)
+    own_change, their_change = (change.astype(BF16) for change in changes())
+    for i, (lo, hi) in enumerate(chunks):
+        for copy in copies[i]:
+            copy.wait()
+        at = slice(lo - rows[0], hi - rows[0])
+        put(lo, hi, get(lo, hi) - (dot_bf16(own_change, x[0, at, :], NT) + dot_bf16(their_change, x[1, at, :], NT)))
+
+
+def first_update_kernel(rows, core_ref, own_ref, other_ref, here_ref, there_ref, residual_ref, new_ref, x, sems):
     core = core_ref[0]
-    shift = jnp.where(core == 0, here_ref[...], there_ref[...])
-    mine_ref[...] = update_rows(0, core, own_ref, other_ref, shift, residual_ref, new_ref, x, sems)
+
+    def put(lo, hi, value):
+        new_ref[:, lo - rows[0] : hi - rows[0]] = value
+
+    update_rows(
+        0, rows, own_ref, other_ref, lambda: halves(jnp.where(core == 0, here_ref[...], there_ref[...]), core),
+        lambda lo, hi: residual_ref[:, lo:hi], put, x, sems,
+    )
 
 
 def last_update_kernel(
-    layout, people, core_ref, own_ref, other_ref, here_ref, there_ref, residual_ref, effects_ref, first_ref, norm_ref,
-    chi_ref, new_ref, new_effects_ref, draw_ref, x, sems
+    layout, people, cut, core_ref, own_ref, other_ref, here_ref, there_ref, low_ref, high_ref, effects_ref,
+    first_here_ref, first_there_ref, norm_ref, chi_ref, new_ref, new_effects_ref, draw_ref, x, sems
 ):
     core, width = core_ref[0], 2 * own_ref.shape[2]
+
+    def changes():
+        mine, theirs = halves(jnp.where(core == 1, here_ref[:, :width], there_ref[:, :width]), core)
+        new_effects_ref[1] = effects_ref[1] + mine
+        return mine, theirs
+
+    def get(lo, hi):
+        return low_ref[:, lo:hi] if lo < cut else high_ref[:, lo - cut : hi - cut]
+
+    def put(lo, hi, value):
+        new_ref[:, lo:hi] = value
+
+    update_rows(1, (0, own_ref.shape[1]), own_ref, other_ref, changes, get, put, x, sems)
+    first = halves(jnp.where(core == 0, first_here_ref[...], first_there_ref[...]), core)[0]
+    new_effects_ref[0] = effects_ref[0] + first
     squares = norm_ref[...] + (here_ref[:, width:] + there_ref[:, width:])
     draw_ref[...] = squares.T[:1, :] / (people * chi_ref[...])
-    shift = jnp.where(core == 1, here_ref[:, :width], there_ref[:, :width])
-    mine = update_rows(1, core, own_ref, other_ref, shift, residual_ref, new_ref, x, sems)
-    new_effects_ref[0] = effects_ref[0] + first_ref[...]
-    new_effects_ref[1] = effects_ref[1] + mine
-
-
-def update_call(kernel, out_shape, genotypes, name, *operands):
-    rows, half = genotypes.shape[1:]
+
+
+def update_call(kernel, out_shape, rows, genotypes, name, *operands):
+    half = genotypes.shape[2]
     return pl.pallas_call(
         kernel,
         out_shape=out_shape,
@@ -515,18 +553,21 @@
 
 def line_sums(value, beside, spots):
     stride = 1
+    beside = list(beside)
+    ready = []
     while stride < spots:
         at = [i // stride % LINE for i in range(spots)]
         one, two, three = (
             lax.ppermute(value, "ind", [(i, i + ((at[i] + step) % LINE - at[i]) * stride) for i in range(spots)])
             for step in range(1, LINE)
         )
-        if stride == 1:
-            one, two, three, beside = lax.optimization_barrier((one, two, three, beside))
+        if beside:
+            one, two, three, done = lax.optimization_barrier((one, two, three, beside.pop(0)))
+            ready.append(done)
         even = lax.axis_index("ind") // stride % 2 == 0
         value = (value + jnp.where(even, three, one)) + (two + jnp.where(even, one, three))
         stride *= LINE
-    return value, beside
+    return value, ready + beside
 
 
 def local(genotypes, residual, effects, noise, prior_var, block_snps, noise_var, chi_scaled):
@@ -651,18 +692,23 @@
         compiler_params=PARAMS,
         name="cross_share",
     )(core_arg, shift, got_shift, cross)
-    after_0, first_shift = update_call(
-        first_update_kernel,
-        (jax.ShapeDtypeStruct(residual.shape, F32), jax.ShapeDtypeStruct((chains, half), F32)),
-        genotypes,
-        "first_update",
-        core_arg,
-        other,
-        shift,
-        got_shift,
-        residual,
-    )
-    share, after_0 = line_sums(share, after_0, spots)
+    cut = rows // 2 // CHUNK * CHUNK + CHUNK if rows > CHUNK else rows
+    after = [
+        update_call(
+            functools.partial(first_update_kernel, part),
+            (jax.ShapeDtypeStruct((chains, part[1] - part[0]), F32),),
+            part[1] - part[0],
+            genotypes,
+            "first_update",
+            core_arg,
+            other,
+            shift,
+            got_shift,
+            residual,
+        )[0]
+        for part in ((0, cut), (cut, rows))
+    ]
+    share, after = line_sums(share, after, spots)
     got = lax.ppermute(share, "snp", swap)
     final = pl.pallas_call(
         functools.partial(second_kernel, layout),
@@ -680,21 +726,23 @@
     )(core_arg, shift, share, got, panels, inverse, packed)
     got_final = lax.ppermute(final, "snp", swap)
     new_residual, new_effects, draw = update_call(
-        functools.partial(last_update_kernel, layout, rows * spots),
+        functools.partial(last_update_kernel, layout, rows * spots, cut),
         (
             jax.ShapeDtypeStruct(residual.shape, F32),
             jax.ShapeDtypeStruct(effects.shape, F32),
             jax.ShapeDtypeStruct((1, chains), F32),
         ),
+        rows,
         genotypes,
         "last_update",
         core_arg,
         other,
         final,
         got_final,
-        after_0,
+        *after,
         effects,
-        first_shift,
+        shift,
+        got_shift,
         packed[layout.squares : layout.used],
         chi_scaled[None, :],
     )

time: 187 us -> 182 us (0.973)
  waiting for transfers between devices: 69.5 us -> 67.6 us
    pallas_call x1, Pallas kernels: 35.7 us -> 32.4 us  [local(): pl.pallas_call(functools.partial(factor_kernel, layout), out_shape=(jax.S...]
    ppermute x9, waiting for transfers between devices: 4.55 us -> 2.66 us  [line_sums(): lax.ppermute(value, 'ind', [(i, i + ((at[i] + step) % LINE - at[i]) * str...]
    pallas_call x2 -> x3, Pallas kernels: 9.81 us -> 11.3 us  [update_call(): pl.pallas_call(kernel, out_shape=out_shape, in_specs=[SMEM, ANY, ANY] + [...]
  transfers between devices with their start and end apart: 16 -> 16, of which waited for: 11 -> 10; matrix products, arithmetic and copies ran while one was open for 0% -> 0% of each run, Pallas kernels for 10% -> 11%
where the time goes in v3:
time: 182 us; the launch traced here: 180 us
  Pallas kernels  77.7 us (43%)
  waiting for transfers between devices  67.6 us (37%)
  starting transfers between devices  32 us (18%)
  local copies, waits for them, and re-layouts  1.93 us (1%)
    pallas_call x1, Pallas kernels, local(): pl.pallas_call(functools.partial(factor_kernel, layout), out_shape=(jax.S...  32.4 us
    all_to_all x1, waiting for transfers between devices, local(): packed = lax.all_to_all(packed, 'ind', 0, 0).reshape(spots * piece, TILE)  29.5 us
    all_to_all x1, waiting for transfers between devices, local(): packed = lax.all_to_all(packed.reshape(spots, piece, TILE), 'ind', 0, 0)  26.9 us
    ppermute x9, starting transfers between devices, line_sums(): lax.ppermute(value, 'ind', [(i, i + ((at[i] + step) % LINE - at[i]) * str...  12.6 us
    all_to_all x1, starting transfers between devices, local(): packed = lax.all_to_all(packed.reshape(spots, piece, TILE), 'ind', 0, 0)  11.9 us
    pallas_call x3, Pallas kernels, update_call(): pl.pallas_call(kernel, out_shape=out_shape, in_specs=[SMEM, ANY, ANY] + [...  11.3 us
    pallas_call x1, Pallas kernels, local(): pl.pallas_call(functools.partial(gram_kernel, layout), out_shape=jax.Shap...  8.93 us
    pallas_call x1, Pallas kernels, local(): pl.pallas_call(own_kernel, out_shape=(jax.ShapeDtypeStruct((half, half),...  7.58 us
  transfers between devices with their start and end apart: 16, of which 10 were waited for; matrix products, arithmetic and copies ran while one was open for 0% of the time, Pallas kernels for 11%

profile of v3, /device:TPU:0, one launch (start us, length us, event | category | flops | bytes accessed | tf_op | source)
XLA Modules:
  0.0 180.5 jit_solution(17690532525364207337)
XLA Ops:
  0.8 1.0 copy-done.1
  1.8 7.6 %own.1 = (f32[512,512]{1,0:T(8,128)S(1)}, f32[32,512]{1,0:T(8,128)S(1)}, f32[512,512]{1,0:T(8,128)}) custom-call(s32[1]{0:T(128)} %bitcast.core_ref, bf16[2,3904,512]{2,1,0:T(8,128)(2,1)} %own_ref.11, f32[32,3904]{1,0:T(8,128)S(1)} %copy-done.1), custom_call_target="tpu_custom_call" | custom-call | flops 2046820352 | bytes 3997696 | tf_op jit(solution)/shard_map/own/pallas_call | solution.py:589
  9.4 4.3 %collective-permute-done.other_ref = bf16[2,3904,512]{2,1,0:T(8,128)(2,1)} collective-permute-done((bf16[2,3904,512]{2,1,0:T(8,128)(2,1)}, bf16[2,3904,512]{2,1,0:T(8,128)(2,1)}, u32[]{:S(2)}, u32[]{:S(2)}) %collective-permute-start) | collective-permute-done | bytes 7995424 | tf_op jit(solution)/shard_map/ppermute | solution.py:584
  13.7 8.9 %gram.1 = f32[4608,128]{1,0:T(8,128)} custom-call(s32[1]{0:T(128)} %bitcast.core_ref, bf16[2,3904,512]{2,1,0:T(8,128)(2,1)} %own_ref.11, bf16[2,3904,512]{2,1,0:T(8,128)(2,1)} %collective-permute-done.other_ref, f32[32,3904]{1,0:T(8,128)S(1)} %copy-done.1, f32[512,512]{1,0:T(8,128)S(1)} %get-tuple-element.24.square_ref, ...), custom_call_target="tpu_custom_call" | custom-call | tf_op jit(solution)/shard_map/gram/pallas_call | solution.py:603
  22.6 11.9 %all-to-all-start = ((f32[64,72,128]{2,1,0:T(8,128)}), f32[64,72,128]{2,1,0:T(8,128)}, u32[]{:S(2)}, u32[]{:S(2)}) async-start(f32[64,72,128]{2,1,0:T(8,128)} %bitcast.19), calls=%async_computation | async-start | bytes 4718592 | tf_op jit(solution)/shard_map/all_to_all | solution.py:633
  34.5 5.9 %cross.1.cross_hbm = f32[2,512,512]{2,1,0:T(8,128)} custom-call(bf16[2,3904,512]{2,1,0:T(8,128)(2,1)} %own_ref.11, bf16[2,3904,512]{2,1,0:T(8,128)(2,1)} %collective-permute-done.other_ref, f32[512,512]{1,0:T(8,128)S(1)} %copy-done.3), custom_call_target="tpu_custom_call" | custom-call | flops 2046820352 | bytes 7995392 | tf_op jit(solution)/shard_map/cross/pallas_call | solution.py:620
  40.4 26.9 %all-to-all-done.parts_ref = f32[64,72,128]{2,1,0:T(8,128)} async-done(((f32[64,72,128]{2,1,0:T(8,128)}), f32[64,72,128]{2,1,0:T(8,128)}, u32[]{:S(2)}, u32[]{:S(2)}) %all-to-all-start) | async-done | bytes 2359328 | tf_op jit(solution)/shard_map/all_to_all | solution.py:633
  67.3 3.2 %sums.1 = f32[64,72,128]{2,1,0:T(8,128)} custom-call(f32[64,72,128]{2,1,0:T(8,128)} %all-to-all-done.parts_ref), custom_call_target="tpu_custom_call" | custom-call | tf_op jit(solution)/shard_map/sums/pallas_call | solution.py:635
  70.5 6.8 %all-to-all-start.1 = ((f32[64,72,128]{2,1,0:T(8,128)}), f32[64,72,128]{2,1,0:T(8,128)}, u32[]{:S(2)}, u32[]{:S(2)}) async-start(f32[64,72,128]{2,1,0:T(8,128)} %sums.1), calls=%async_computation.1 | async-start | bytes 4718592 | tf_op jit(solution)/shard_map/all_to_all | solution.py:649
  77.8 1.2 collective-permute-done.1
  79.0 29.5 %all-to-all-done.1 = f32[64,72,128]{2,1,0:T(8,128)} async-done(((f32[64,72,128]{2,1,0:T(8,128)}), f32[64,72,128]{2,1,0:T(8,128)}, u32[]{:S(2)}, u32[]{:S(2)}) %all-to-all-start.1) | async-done | bytes 2359328 | tf_op jit(solution)/shard_map/all_to_all | solution.py:649
  108.5 32.4 %factor.1 = (f32[1536,256]{1,0:T(8,128)}, f32[4,256,256]{2,1,0:T(8,128)S(1)}, f32[32,1024]{1,0:T(8,128)S(1)}) custom-call(f32[4608,128]{1,0:T(8,128)} %bitcast.2.packed_hbm, f32[16,128]{1,0:T(8,128)S(1)} %bitcast.17, s32[8,128]{1,0:T(8,128)S(1)} %dynamic-slice_bitcast_fusion.3.rows_ref, f32[32,1024]{1,0:T(8,128)S(1)} %maximum_select_fusion.effects_ref, ...), custom_call_target="tpu_custom_call" | custom-call | tf_op jit(solution)/shard_map/factor/pallas_call | solution.py:663
  141.0 1.3 collective-permute-done.2.got_ref.there_ref.first_there_ref
  142.3 2.0 %cross_share.1 = f32[32,512]{1,0:T(8,128)S(1)} custom-call(s32[1]{0:T(128)} %bitcast.core_ref, f32[32,1024]{1,0:T(8,128)S(1)} %get-tuple-element.30.shift_ref.here_ref.first_here_ref, f32[32,1024]{1,0:T(8,128)S(1)} %collective-permute-done.2.got_ref.there_ref.first_there_ref, f32[2,512,512]{2,1,0:T(8,128)} %cross.1.cross_hbm), custom_call_target="tpu_custom_call" | custom-call | tf_op jit(solution)/shard_map/cross_share/pallas_call | solution.py:686
  144.4 1.0 collective-permute-start.3
  145.4 1.3 collective-permute-start.4
  146.7 2.2 %collective-permute-start.5 = (f32[32,512]{1,0:T(8,128)S(1)}, f32[32,512]{1,0:T(8,128)S(1)}, u32[]{:S(2)}, u32[]{:S(2)}) collective-permute-start(f32[32,512]{1,0:T(8,128)S(1)} %cross_share.1), channel_id=1, source_target_pairs={{0,6},{2,0},{4,2},{6,4},{8,14},{10,8},{12,10},{14,12},{16,22},{18,... | collective-permute-start | bytes 196616 | tf_op jit(solution)/shard_map/ppermute | solution.py:561
  148.9 3.0 %first_update.2.low_ref = f32[32,2048]{1,0:T(8,128)S(1)} custom-call(s32[1]{0:T(128)} %bitcast.core_ref, bf16[2,3904,512]{2,1,0:T(8,128)(2,1)} %own_ref.11, bf16[2,3904,512]{2,1,0:T(8,128)(2,1)} %collective-permute-done.other_ref, f32[32,1024]{1,0:T(8,128)S(1)} %get-tuple-element.30.shift_ref.here_ref.first_here_ref, ...), custom_call_target="tpu_custom_call" | custom-call | flops 536870912 | bytes 4194304 | tf_op jit(solution)/shard_map/first_update/pallas_call | solution.py:539
  152.0 0.7 collective-permute-start.6
  152.7 1.6 collective-permute-start.7
  154.2 1.4 collective-permute-start.8
  155.6 3.0 %first_update.3.high_ref = f32[32,1856]{1,0:T(8,128)S(1)} custom-call(s32[1]{0:T(128)} %bitcast.core_ref, bf16[2,3904,512]{2,1,0:T(8,128)(2,1)} %own_ref.11, bf16[2,3904,512]{2,1,0:T(8,128)(2,1)} %collective-permute-done.other_ref, f32[32,1024]{1,0:T(8,128)S(1)} %get-tuple-element.30.shift_ref.here_ref.first_here_ref, ...), custom_call_target="tpu_custom_call" | custom-call | flops 486539264 | bytes 3801088 | tf_op jit(solution)/shard_map/first_update/pallas_call | solution.py:539
  159.1 1.2 collective-permute-start.11
  160.3 0.8 collective-permute-start.10
  161.1 2.4 %collective-permute-start.9 = (f32[32,512]{1,0:T(8,128)S(1)}, f32[32,512]{1,0:T(8,128)S(1)}, u32[]{:S(2)}, u32[]{:S(2)}) collective-permute-start(f32[32,512]{1,0:T(8,128)S(1)} %add_add_fusion.1), channel_id=1, source_target_pairs={{0,96},{2,98},{4,100},{6,102},{8,104},{10,106},{12,108},{14,110},{... | collective-permute-start | bytes 196616 | tf_op jit(solution)/shard_map/ppermute | solution.py:561
  163.5 1.4 collective-permute-done.11
  165.0 0.8 collective-permute-done.10
  165.9 1.2 collective-permute-done.12.got_ref
  167.1 6.4 %second.1.here_ref = f32[32,1152]{1,0:T(8,128)S(1)} custom-call(s32[1]{0:T(128)} %bitcast.core_ref, f32[32,1024]{1,0:T(8,128)S(1)} %get-tuple-element.30.shift_ref.here_ref.first_here_ref, f32[32,512]{1,0:T(8,128)S(1)} %add_add_fusion.share_ref, f32[32,512]{1,0:T(8,128)S(1)} %collective-permute-done.12.got_ref, f32[1536,256]{1,0:T(8,128)} %get-tuple-element.38.panels_hbm, ...), custom_call_target="tpu_custom_call" | custom-call | tf_op jit(solution)/shard_map/second/pallas_call | solution.py:713
  173.8 0.7 slice.4.norm_ref
  174.5 0.5 collective-permute-done.13.there_ref
  175.0 5.3 %last_update.1 = (f32[32,3904]{1,0:T(8,128)}, f32[2,32,512]{2,1,0:T(8,128)}, f32[1,32]{1,0:T(1,128)}) custom-call(s32[1]{0:T(128)} %bitcast.core_ref, bf16[2,3904,512]{2,1,0:T(8,128)(2,1)} %own_ref.11, bf16[2,3904,512]{2,1,0:T(8,128)(2,1)} %collective-permute-done.other_ref, f32[32,1152]{1,0:T(8,128)S(1)} %second.1.here_ref, ...), custom_call_target="tpu_custom_call" | custom-call | flops 1023410176 | bytes 7995392 | tf_op jit(solution)/shard_map/last_update/pallas_call | solution.py:539
  (39 shorter events, 1.4 us)
Async XLA Ops:
  0.6 77.2 %copy-start = (f32[2,32,1024]{2,1,0:T(8,128)S(1)}, f32[2,32,1024]{2,1,0:T(8,128)}, u32[]{:S(2)}) copy-start(f32[2,32,1024]{2,1,0:T(8,128)} %param.11) | copy-start | bytes 786436
  0.6 13.0 %collective-permute-start = (bf16[2,3904,512]{2,1,0:T(8,128)(2,1)}, bf16[2,3904,512]{2,1,0:T(8,128)(2,1)}, u32[]{:S(2)}, u32[]{:S(2)}) collective-permute-start(bf16[2,3904,512]{2,1,0:T(8,128)(2,1)} %own_ref.11), channel_id=1, source_target_pairs={{0,1},{1,0},{2,3},{3,2},{4,5},{5,4},{6,7},{7,6},{8,9},{9,8},{10,11... | collective-permute-start | bytes 23986184 | tf_op jit(solution)/shard_map/ppermute | solution.py:584
  0.7 1.0 copy-start.1
  22.6 11.9 %copy-start.3 = (f32[512,512]{1,0:T(8,128)S(1)}, f32[512,512]{1,0:T(8,128)}, u32[]{:S(2)}) copy-start(f32[512,512]{1,0:T(8,128)} %get-tuple-element.28.own_cross_ref) | copy-start | bytes 3145732
  22.6 44.7 %all-to-all-start = ((f32[64,72,128]{2,1,0:T(8,128)}), f32[64,72,128]{2,1,0:T(8,128)}, u32[]{:S(2)}, u32[]{:S(2)}) async-start(f32[64,72,128]{2,1,0:T(8,128)} %bitcast.19), calls=%async_computation | async-start | bytes 4718592 | tf_op jit(solution)/shard_map/all_to_all | solution.py:633
  70.5 6.9 %copy-start.4 = (f32[2,32,512]{2,1,0:T(8,128)S(1)}, f32[2,32,512]{2,1,0:T(8,128)}, u32[]{:S(2)}) copy-start(f32[2,32,512]{2,1,0:T(8,128)} %effects_ref.1) | copy-start | bytes 393220
  70.5 7.2 %copy-start.8 = (f32[32]{0:T(128)S(1)}, f32[32]{0:T(128)}, u32[]{:S(2)}) copy-start(f32[32]{0:T(128)} %param.14) | copy-start | bytes 388
  70.5 7.2 %copy-start.7 = (s32[2048]{0:T(1024)S(1)}, s32[2048]{0:T(1024)}, u32[]{:S(2)}) copy-start(s32[2048]{0:T(1024)} %param.13) | copy-start | bytes 24580
  70.5 38.0 %copy-start.5 = (f32[2048]{0:T(1024)S(1)}, f32[2048]{0:T(1024)}, u32[]{:S(2)}) copy-start(f32[2048]{0:T(1024)} %param.12) | copy-start | bytes 24580
  70.5 38.0 %all-to-all-start.1 = ((f32[64,72,128]{2,1,0:T(8,128)}), f32[64,72,128]{2,1,0:T(8,128)}, u32[]{:S(2)}, u32[]{:S(2)}) async-start(f32[64,72,128]{2,1,0:T(8,128)} %sums.1), calls=%async_computation.1 | async-start | bytes 4718592 | tf_op jit(solution)/shard_map/all_to_all | solution.py:649
  77.4 1.6 collective-permute-start.1
  108.5 40.4 %copy-start.2 = (f32[32,3904]{1,0:T(8,128)S(1)}, f32[32,3904]{1,0:T(8,128)}, u32[]{:S(2)}) copy-start(f32[32,3904]{1,0:T(8,128)} %residual_ref.7) | copy-start | bytes 1499140
  140.9 1.4 collective-permute-start.2
  144.4 7.6 %collective-permute-start.3 = (f32[32,512]{1,0:T(8,128)S(1)}, f32[32,512]{1,0:T(8,128)S(1)}, u32[]{:S(2)}, u32[]{:S(2)}) collective-permute-start(f32[32,512]{1,0:T(8,128)S(1)} %cross_share.1), channel_id=1, source_target_pairs={{0,2},{2,4},{4,6},{6,0},{8,10},{10,12},{12,14},{14,8},{16,18},{18,... | collective-permute-start | bytes 196616 | tf_op jit(solution)/shard_map/ppermute | solution.py:561
  145.4 6.5 %collective-permute-start.4 = (f32[32,512]{1,0:T(8,128)S(1)}, f32[32,512]{1,0:T(8,128)S(1)}, u32[]{:S(2)}, u32[]{:S(2)}) collective-permute-start(f32[32,512]{1,0:T(8,128)S(1)} %cross_share.1), channel_id=1, source_target_pairs={{0,4},{2,6},{4,0},{6,2},{8,12},{10,14},{12,8},{14,10},{16,20},{18,... | collective-permute-start | bytes 196616 | tf_op jit(solution)/shard_map/ppermute | solution.py:561
  146.7 5.2 %collective-permute-start.5 = (f32[32,512]{1,0:T(8,128)S(1)}, f32[32,512]{1,0:T(8,128)S(1)}, u32[]{:S(2)}, u32[]{:S(2)}) collective-permute-start(f32[32,512]{1,0:T(8,128)S(1)} %cross_share.1), channel_id=1, source_target_pairs={{0,6},{2,0},{4,2},{6,4},{8,14},{10,8},{12,10},{14,12},{16,22},{18,... | collective-permute-start | bytes 196616 | tf_op jit(solution)/shard_map/ppermute | solution.py:561
  152.0 6.7 %collective-permute-start.6 = (f32[32,512]{1,0:T(8,128)S(1)}, f32[32,512]{1,0:T(8,128)S(1)}, u32[]{:S(2)}, u32[]{:S(2)}) collective-permute-start(f32[32,512]{1,0:T(8,128)S(1)} %add_add_fusion.2), channel_id=1, source_target_pairs={{0,8},{2,10},{4,12},{6,14},{8,16},{10,18},{12,20},{14,22},{16,24},... | collective-permute-start | bytes 196616 | tf_op jit(solution)/shard_map/ppermute | solution.py:561
  152.7 6.0 %collective-permute-start.7 = (f32[32,512]{1,0:T(8,128)S(1)}, f32[32,512]{1,0:T(8,128)S(1)}, u32[]{:S(2)}, u32[]{:S(2)}) collective-permute-start(f32[32,512]{1,0:T(8,128)S(1)} %add_add_fusion.2), channel_id=1, source_target_pairs={{0,16},{2,18},{4,20},{6,22},{8,24},{10,26},{12,28},{14,30},{16,0},... | collective-permute-start | bytes 196616 | tf_op jit(solution)/shard_map/ppermute | solution.py:561
  154.2 4.9 %collective-permute-start.8 = (f32[32,512]{1,0:T(8,128)S(1)}, f32[32,512]{1,0:T(8,128)S(1)}, u32[]{:S(2)}, u32[]{:S(2)}) collective-permute-start(f32[32,512]{1,0:T(8,128)S(1)} %add_add_fusion.2), channel_id=1, source_target_pairs={{0,24},{2,26},{4,28},{6,30},{8,0},{10,2},{12,4},{14,6},{16,8},{18,... | collective-permute-start | bytes 196616 | tf_op jit(solution)/shard_map/ppermute | solution.py:561
  159.1 5.8 %collective-permute-start.11 = (f32[32,512]{1,0:T(8,128)S(1)}, f32[32,512]{1,0:T(8,128)S(1)}, u32[]{:S(2)}, u32[]{:S(2)}) collective-permute-start(f32[32,512]{1,0:T(8,128)S(1)} %add_add_fusion.1), channel_id=1, source_target_pairs={{0,64},{2,66},{4,68},{6,70},{8,72},{10,74},{12,76},{14,78},{16,80}... | collective-permute-start | bytes 196616 | tf_op jit(solution)/shard_map/ppermute | solution.py:561
  160.3 5.5 %collective-permute-start.10 = (f32[32,512]{1,0:T(8,128)S(1)}, f32[32,512]{1,0:T(8,128)S(1)}, u32[]{:S(2)}, u32[]{:S(2)}) collective-permute-start(f32[32,512]{1,0:T(8,128)S(1)} %add_add_fusion.1), channel_id=1, source_target_pairs={{0,32},{2,34},{4,36},{6,38},{8,40},{10,42},{12,44},{14,46},{16,48}... | collective-permute-start | bytes 196616 | tf_op jit(solution)/shard_map/ppermute | solution.py:561
  161.1 4.6 %collective-permute-start.9 = (f32[32,512]{1,0:T(8,128)S(1)}, f32[32,512]{1,0:T(8,128)S(1)}, u32[]{:S(2)}, u32[]{:S(2)}) collective-permute-start(f32[32,512]{1,0:T(8,128)S(1)} %add_add_fusion.1), channel_id=1, source_target_pairs={{0,96},{2,98},{4,100},{6,102},{8,104},{10,106},{12,108},{14,110},{... | collective-permute-start | bytes 196616 | tf_op jit(solution)/shard_map/ppermute | solution.py:561
  165.8 1.3 collective-permute-start.12
  167.1 7.9 %copy-start.6 = (f32[32]{0:T(128)S(1)}, f32[32]{0:T(128)}, u32[]{:S(2)}) copy-start(f32[32]{0:T(128)} %param.15) | copy-start | bytes 388
  173.5 1.5 collective-permute-start.13

commit v4 on v3

--- a/solution.py
+++ b/solution.py
@@ -478,24 +478,25 @@
 
 
 def update_rows(block, rows, own_ref, other_ref, changes, get, put, x, sems):
+    half = own_ref.shape[2]
     chunks = [(lo, min(lo + CHUNK, rows[1])) for lo in range(rows[0], rows[1], CHUNK)]
     copies = []
     for i, (lo, hi) in enumerate(chunks):
         pair = [
             pltpu.make_async_copy(
-                source.at[block, lo:hi, :], x.at[k, lo - rows[0] : hi - rows[0], :], sems.at[i, k]
+                source.at[block, lo:hi, :], x.at[lo - rows[0] : hi - rows[0], k * half : (k + 1) * half], sems.at[i, k]
             )
             for k, source in enumerate((own_ref, other_ref))
         ]
         for copy in pair:
             copy.start()
         copies.append(pair)
-    own_change, their_change = (change.astype(BF16) for change in changes())
+    change = jnp.concatenate(changes(), axis=1).astype(BF16)
     for i, (lo, hi) in enumerate(chunks):
         for copy in copies[i]:
             copy.wait()
         at = slice(lo - rows[0], hi - rows[0])
-        put(lo, hi, get(lo, hi) - (dot_bf16(own_change, x[0, at, :], NT) + dot_bf16(their_change, x[1, at, :], NT)))
+        put(lo, hi, get(lo, hi) - dot_bf16(change, x[at, :], NT))
 
 
 def first_update_kernel(rows, core_ref, own_ref, other_ref, here_ref, there_ref, residual_ref, new_ref, x, sems):
@@ -542,7 +543,7 @@
         in_specs=[SMEM, ANY, ANY] + [VMEM] * (len(operands) - 2),
         out_specs=(VMEM,) * len(out_shape),
         scratch_shapes=[
-            pltpu.VMEM((2, rows, half), BF16),
+            pltpu.VMEM((rows, 2 * half), BF16),
             pltpu.SemaphoreType.DMA((-(-rows // CHUNK), 2)),
         ],
         compiler_params=PARAMS,

time: 182 us -> 182 us (level)
  no operation moved by 1% of the time
where the time goes in v4:
time: 182 us; the launch traced here: 181 us
  Pallas kernels  77.8 us (43%)
  waiting for transfers between devices  67.6 us (37%)
  starting transfers between devices  32 us (18%)
  local copies, waits for them, and re-layouts  1.93 us (1%)
    pallas_call x1, Pallas kernels, local(): pl.pallas_call(functools.partial(factor_kernel, layout), out_shape=(jax.S...  32.4 us
    all_to_all x1, waiting for transfers between devices, local(): packed = lax.all_to_all(packed, 'ind', 0, 0).reshape(spots * piece, TILE)  29.5 us
    all_to_all x1, waiting for transfers between devices, local(): packed = lax.all_to_all(packed.reshape(spots, piece, TILE), 'ind', 0, 0)  26.9 us
    ppermute x9, starting transfers between devices, line_sums(): lax.ppermute(value, 'ind', [(i, i + ((at[i] + step) % LINE - at[i]) * str...  12.6 us
    all_to_all x1, starting transfers between devices, local(): packed = lax.all_to_all(packed.reshape(spots, piece, TILE), 'ind', 0, 0)  11.9 us
    pallas_call x3, Pallas kernels, update_call(): pl.pallas_call(kernel, out_shape=out_shape, in_specs=[SMEM, ANY, ANY] + [...  11.4 us
    pallas_call x1, Pallas kernels, local(): pl.pallas_call(functools.partial(gram_kernel, layout), out_shape=jax.Shap...  8.93 us
    pallas_call x1, Pallas kernels, local(): pl.pallas_call(own_kernel, out_shape=(jax.ShapeDtypeStruct((half, half),...  7.58 us
  transfers between devices with their start and end apart: 16, of which 10 were waited for; matrix products, arithmetic and copies ran while one was open for 0% of the time, Pallas kernels for 11%

profile of v4, /device:TPU:0, one launch (start us, length us, event | category | flops | bytes accessed | tf_op | source)
XLA Modules:
  0.0 180.5 jit_solution(1685291851755371512)
XLA Ops:
  0.8 1.0 copy-done.1
  1.8 7.6 %own.1 = (f32[512,512]{1,0:T(8,128)S(1)}, f32[32,512]{1,0:T(8,128)S(1)}, f32[512,512]{1,0:T(8,128)}) custom-call(s32[1]{0:T(128)} %bitcast.core_ref, bf16[2,3904,512]{2,1,0:T(8,128)(2,1)} %own_ref.11, f32[32,3904]{1,0:T(8,128)S(1)} %copy-done.1), custom_call_target="tpu_custom_call" | custom-call | flops 2046820352 | bytes 3997696 | tf_op jit(solution)/shard_map/own/pallas_call | solution.py:590
  9.4 4.3 %collective-permute-done.other_ref = bf16[2,3904,512]{2,1,0:T(8,128)(2,1)} collective-permute-done((bf16[2,3904,512]{2,1,0:T(8,128)(2,1)}, bf16[2,3904,512]{2,1,0:T(8,128)(2,1)}, u32[]{:S(2)}, u32[]{:S(2)}) %collective-permute-start) | collective-permute-done | bytes 7995424 | tf_op jit(solution)/shard_map/ppermute | solution.py:585
  13.7 8.9 %gram.1 = f32[4608,128]{1,0:T(8,128)} custom-call(s32[1]{0:T(128)} %bitcast.core_ref, bf16[2,3904,512]{2,1,0:T(8,128)(2,1)} %own_ref.11, bf16[2,3904,512]{2,1,0:T(8,128)(2,1)} %collective-permute-done.other_ref, f32[32,3904]{1,0:T(8,128)S(1)} %copy-done.1, f32[512,512]{1,0:T(8,128)S(1)} %get-tuple-element.24.square_ref, ...), custom_call_target="tpu_custom_call" | custom-call | tf_op jit(solution)/shard_map/gram/pallas_call | solution.py:604
  22.6 11.9 %all-to-all-start = ((f32[64,72,128]{2,1,0:T(8,128)}), f32[64,72,128]{2,1,0:T(8,128)}, u32[]{:S(2)}, u32[]{:S(2)}) async-start(f32[64,72,128]{2,1,0:T(8,128)} %bitcast.19), calls=%async_computation | async-start | bytes 4718592 | tf_op jit(solution)/shard_map/all_to_all | solution.py:634
  34.5 5.9 %cross.1.cross_hbm = f32[2,512,512]{2,1,0:T(8,128)} custom-call(bf16[2,3904,512]{2,1,0:T(8,128)(2,1)} %own_ref.11, bf16[2,3904,512]{2,1,0:T(8,128)(2,1)} %collective-permute-done.other_ref, f32[512,512]{1,0:T(8,128)S(1)} %copy-done.3), custom_call_target="tpu_custom_call" | custom-call | flops 2046820352 | bytes 7995392 | tf_op jit(solution)/shard_map/cross/pallas_call | solution.py:621
  40.4 26.9 %all-to-all-done.parts_ref = f32[64,72,128]{2,1,0:T(8,128)} async-done(((f32[64,72,128]{2,1,0:T(8,128)}), f32[64,72,128]{2,1,0:T(8,128)}, u32[]{:S(2)}, u32[]{:S(2)}) %all-to-all-start) | async-done | bytes 2359328 | tf_op jit(solution)/shard_map/all_to_all | solution.py:634
  67.3 3.2 %sums.1 = f32[64,72,128]{2,1,0:T(8,128)} custom-call(f32[64,72,128]{2,1,0:T(8,128)} %all-to-all-done.parts_ref), custom_call_target="tpu_custom_call" | custom-call | tf_op jit(solution)/shard_map/sums/pallas_call | solution.py:636
  70.5 6.8 %all-to-all-start.1 = ((f32[64,72,128]{2,1,0:T(8,128)}), f32[64,72,128]{2,1,0:T(8,128)}, u32[]{:S(2)}, u32[]{:S(2)}) async-start(f32[64,72,128]{2,1,0:T(8,128)} %sums.1), calls=%async_computation.1 | async-start | bytes 4718592 | tf_op jit(solution)/shard_map/all_to_all | solution.py:650
  77.8 1.2 collective-permute-done.1
  79.0 29.5 %all-to-all-done.1 = f32[64,72,128]{2,1,0:T(8,128)} async-done(((f32[64,72,128]{2,1,0:T(8,128)}), f32[64,72,128]{2,1,0:T(8,128)}, u32[]{:S(2)}, u32[]{:S(2)}) %all-to-all-start.1) | async-done | bytes 2359328 | tf_op jit(solution)/shard_map/all_to_all | solution.py:650
  108.5 32.4 %factor.1 = (f32[1536,256]{1,0:T(8,128)}, f32[4,256,256]{2,1,0:T(8,128)S(1)}, f32[32,1024]{1,0:T(8,128)S(1)}) custom-call(f32[4608,128]{1,0:T(8,128)} %bitcast.2.packed_hbm, f32[16,128]{1,0:T(8,128)S(1)} %bitcast.17, s32[8,128]{1,0:T(8,128)S(1)} %dynamic-slice_bitcast_fusion.3.rows_ref, f32[32,1024]{1,0:T(8,128)S(1)} %maximum_select_fusion.effects_ref, ...), custom_call_target="tpu_custom_call" | custom-call | tf_op jit(solution)/shard_map/factor/pallas_call | solution.py:664
  141.0 1.3 collective-permute-done.2.got_ref.there_ref.first_there_ref
  142.3 2.0 %cross_share.1 = f32[32,512]{1,0:T(8,128)S(1)} custom-call(s32[1]{0:T(128)} %bitcast.core_ref, f32[32,1024]{1,0:T(8,128)S(1)} %get-tuple-element.30.shift_ref.here_ref.first_here_ref, f32[32,1024]{1,0:T(8,128)S(1)} %collective-permute-done.2.got_ref.there_ref.first_there_ref, f32[2,512,512]{2,1,0:T(8,128)} %cross.1.cross_hbm), custom_call_target="tpu_custom_call" | custom-call | tf_op jit(solution)/shard_map/cross_share/pallas_call | solution.py:687
  144.4 1.0 collective-permute-start.3
  145.4 1.3 collective-permute-start.4
  146.7 2.2 %collective-permute-start.5 = (f32[32,512]{1,0:T(8,128)S(1)}, f32[32,512]{1,0:T(8,128)S(1)}, u32[]{:S(2)}, u32[]{:S(2)}) collective-permute-start(f32[32,512]{1,0:T(8,128)S(1)} %cross_share.1), channel_id=1, source_target_pairs={{0,6},{2,0},{4,2},{6,4},{8,14},{10,8},{12,10},{14,12},{16,22},{18,... | collective-permute-start | bytes 196616 | tf_op jit(solution)/shard_map/ppermute | solution.py:562
  148.9 3.0 %first_update.2.low_ref = f32[32,2048]{1,0:T(8,128)S(1)} custom-call(s32[1]{0:T(128)} %bitcast.core_ref, bf16[2,3904,512]{2,1,0:T(8,128)(2,1)} %own_ref.11, bf16[2,3904,512]{2,1,0:T(8,128)(2,1)} %collective-permute-done.other_ref, f32[32,1024]{1,0:T(8,128)S(1)} %get-tuple-element.30.shift_ref.here_ref.first_here_ref, ...), custom_call_target="tpu_custom_call" | custom-call | flops 536870912 | bytes 4194304 | tf_op jit(solution)/shard_map/first_update/pallas_call | solution.py:540
  152.0 0.7 collective-permute-start.6
  152.7 1.6 collective-permute-start.7
  154.2 1.4 collective-permute-start.8
  155.6 3.1 %first_update.3.high_ref = f32[32,1856]{1,0:T(8,128)S(1)} custom-call(s32[1]{0:T(128)} %bitcast.core_ref, bf16[2,3904,512]{2,1,0:T(8,128)(2,1)} %own_ref.11, bf16[2,3904,512]{2,1,0:T(8,128)(2,1)} %collective-permute-done.other_ref, f32[32,1024]{1,0:T(8,128)S(1)} %get-tuple-element.30.shift_ref.here_ref.first_here_ref, ...), custom_call_target="tpu_custom_call" | custom-call | flops 486539264 | bytes 3801088 | tf_op jit(solution)/shard_map/first_update/pallas_call | solution.py:540
  159.1 1.2 collective-permute-start.11
  160.3 0.8 collective-permute-start.10
  161.1 2.4 %collective-permute-start.9 = (f32[32,512]{1,0:T(8,128)S(1)}, f32[32,512]{1,0:T(8,128)S(1)}, u32[]{:S(2)}, u32[]{:S(2)}) collective-permute-start(f32[32,512]{1,0:T(8,128)S(1)} %add_add_fusion.1), channel_id=1, source_target_pairs={{0,96},{2,98},{4,100},{6,102},{8,104},{10,106},{12,108},{14,110},{... | collective-permute-start | bytes 196616 | tf_op jit(solution)/shard_map/ppermute | solution.py:562
  163.5 1.4 collective-permute-done.11
  165.0 0.8 collective-permute-done.10
  165.9 1.2 collective-permute-done.12.got_ref
  167.2 6.4 %second.1.here_ref = f32[32,1152]{1,0:T(8,128)S(1)} custom-call(s32[1]{0:T(128)} %bitcast.core_ref, f32[32,1024]{1,0:T(8,128)S(1)} %get-tuple-element.30.shift_ref.here_ref.first_here_ref, f32[32,512]{1,0:T(8,128)S(1)} %add_add_fusion.share_ref, f32[32,512]{1,0:T(8,128)S(1)} %collective-permute-done.12.got_ref, f32[1536,256]{1,0:T(8,128)} %get-tuple-element.38.panels_hbm, ...), custom_call_target="tpu_custom_call" | custom-call | tf_op jit(solution)/shard_map/second/pallas_call | solution.py:714
  173.8 0.7 slice.4.norm_ref
  174.5 0.5 collective-permute-done.13.there_ref
  175.0 5.3 %last_update.1 = (f32[32,3904]{1,0:T(8,128)}, f32[2,32,512]{2,1,0:T(8,128)}, f32[1,32]{1,0:T(1,128)}) custom-call(s32[1]{0:T(128)} %bitcast.core_ref, bf16[2,3904,512]{2,1,0:T(8,128)(2,1)} %own_ref.11, bf16[2,3904,512]{2,1,0:T(8,128)(2,1)} %collective-permute-done.other_ref, f32[32,1152]{1,0:T(8,128)S(1)} %second.1.here_ref, ...), custom_call_target="tpu_custom_call" | custom-call | flops 1023410176 | bytes 7995392 | tf_op jit(solution)/shard_map/last_update/pallas_call | solution.py:540
  (39 shorter events, 1.4 us)
Async XLA Ops:
  0.6 77.2 %copy-start = (f32[2,32,1024]{2,1,0:T(8,128)S(1)}, f32[2,32,1024]{2,1,0:T(8,128)}, u32[]{:S(2)}) copy-start(f32[2,32,1024]{2,1,0:T(8,128)} %param.11) | copy-start | bytes 786436
  0.6 13.0 %collective-permute-start = (bf16[2,3904,512]{2,1,0:T(8,128)(2,1)}, bf16[2,3904,512]{2,1,0:T(8,128)(2,1)}, u32[]{:S(2)}, u32[]{:S(2)}) collective-permute-start(bf16[2,3904,512]{2,1,0:T(8,128)(2,1)} %own_ref.11), channel_id=1, source_target_pairs={{0,1},{1,0},{2,3},{3,2},{4,5},{5,4},{6,7},{7,6},{8,9},{9,8},{10,11... | collective-permute-start | bytes 23986184 | tf_op jit(solution)/shard_map/ppermute | solution.py:585
  0.7 1.0 copy-start.1
  22.6 11.9 %copy-start.3 = (f32[512,512]{1,0:T(8,128)S(1)}, f32[512,512]{1,0:T(8,128)}, u32[]{:S(2)}) copy-start(f32[512,512]{1,0:T(8,128)} %get-tuple-element.28.own_cross_ref) | copy-start | bytes 3145732
  22.6 44.7 %all-to-all-start = ((f32[64,72,128]{2,1,0:T(8,128)}), f32[64,72,128]{2,1,0:T(8,128)}, u32[]{:S(2)}, u32[]{:S(2)}) async-start(f32[64,72,128]{2,1,0:T(8,128)} %bitcast.19), calls=%async_computation | async-start | bytes 4718592 | tf_op jit(solution)/shard_map/all_to_all | solution.py:634
  70.5 6.9 %copy-start.4 = (f32[2,32,512]{2,1,0:T(8,128)S(1)}, f32[2,32,512]{2,1,0:T(8,128)}, u32[]{:S(2)}) copy-start(f32[2,32,512]{2,1,0:T(8,128)} %effects_ref.1) | copy-start | bytes 393220
  70.5 7.2 %copy-start.8 = (f32[32]{0:T(128)S(1)}, f32[32]{0:T(128)}, u32[]{:S(2)}) copy-start(f32[32]{0:T(128)} %param.14) | copy-start | bytes 388
  70.5 7.2 %copy-start.7 = (s32[2048]{0:T(1024)S(1)}, s32[2048]{0:T(1024)}, u32[]{:S(2)}) copy-start(s32[2048]{0:T(1024)} %param.13) | copy-start | bytes 24580
  70.5 38.0 %copy-start.5 = (f32[2048]{0:T(1024)S(1)}, f32[2048]{0:T(1024)}, u32[]{:S(2)}) copy-start(f32[2048]{0:T(1024)} %param.12) | copy-start | bytes 24580
  70.5 38.0 %all-to-all-start.1 = ((f32[64,72,128]{2,1,0:T(8,128)}), f32[64,72,128]{2,1,0:T(8,128)}, u32[]{:S(2)}, u32[]{:S(2)}) async-start(f32[64,72,128]{2,1,0:T(8,128)} %sums.1), calls=%async_computation.1 | async-start | bytes 4718592 | tf_op jit(solution)/shard_map/all_to_all | solution.py:650
  77.4 1.6 collective-permute-start.1
  108.5 40.4 %copy-start.2 = (f32[32,3904]{1,0:T(8,128)S(1)}, f32[32,3904]{1,0:T(8,128)}, u32[]{:S(2)}) copy-start(f32[32,3904]{1,0:T(8,128)} %residual_ref.7) | copy-start | bytes 1499140
  140.9 1.4 collective-permute-start.2
  144.4 7.6 %collective-permute-start.3 = (f32[32,512]{1,0:T(8,128)S(1)}, f32[32,512]{1,0:T(8,128)S(1)}, u32[]{:S(2)}, u32[]{:S(2)}) collective-permute-start(f32[32,512]{1,0:T(8,128)S(1)} %cross_share.1), channel_id=1, source_target_pairs={{0,2},{2,4},{4,6},{6,0},{8,10},{10,12},{12,14},{14,8},{16,18},{18,... | collective-permute-start | bytes 196616 | tf_op jit(solution)/shard_map/ppermute | solution.py:562
  145.4 6.6 %collective-permute-start.4 = (f32[32,512]{1,0:T(8,128)S(1)}, f32[32,512]{1,0:T(8,128)S(1)}, u32[]{:S(2)}, u32[]{:S(2)}) collective-permute-start(f32[32,512]{1,0:T(8,128)S(1)} %cross_share.1), channel_id=1, source_target_pairs={{0,4},{2,6},{4,0},{6,2},{8,12},{10,14},{12,8},{14,10},{16,20},{18,... | collective-permute-start | bytes 196616 | tf_op jit(solution)/shard_map/ppermute | solution.py:562
  146.7 5.2 %collective-permute-start.5 = (f32[32,512]{1,0:T(8,128)S(1)}, f32[32,512]{1,0:T(8,128)S(1)}, u32[]{:S(2)}, u32[]{:S(2)}) collective-permute-start(f32[32,512]{1,0:T(8,128)S(1)} %cross_share.1), channel_id=1, source_target_pairs={{0,6},{2,0},{4,2},{6,4},{8,14},{10,8},{12,10},{14,12},{16,22},{18,... | collective-permute-start | bytes 196616 | tf_op jit(solution)/shard_map/ppermute | solution.py:562
  152.0 6.7 %collective-permute-start.6 = (f32[32,512]{1,0:T(8,128)S(1)}, f32[32,512]{1,0:T(8,128)S(1)}, u32[]{:S(2)}, u32[]{:S(2)}) collective-permute-start(f32[32,512]{1,0:T(8,128)S(1)} %add_add_fusion.2), channel_id=1, source_target_pairs={{0,8},{2,10},{4,12},{6,14},{8,16},{10,18},{12,20},{14,22},{16,24},... | collective-permute-start | bytes 196616 | tf_op jit(solution)/shard_map/ppermute | solution.py:562
  152.7 6.1 %collective-permute-start.7 = (f32[32,512]{1,0:T(8,128)S(1)}, f32[32,512]{1,0:T(8,128)S(1)}, u32[]{:S(2)}, u32[]{:S(2)}) collective-permute-start(f32[32,512]{1,0:T(8,128)S(1)} %add_add_fusion.2), channel_id=1, source_target_pairs={{0,16},{2,18},{4,20},{6,22},{8,24},{10,26},{12,28},{14,30},{16,0},... | collective-permute-start | bytes 196616 | tf_op jit(solution)/shard_map/ppermute | solution.py:562
  154.2 4.9 %collective-permute-start.8 = (f32[32,512]{1,0:T(8,128)S(1)}, f32[32,512]{1,0:T(8,128)S(1)}, u32[]{:S(2)}, u32[]{:S(2)}) collective-permute-start(f32[32,512]{1,0:T(8,128)S(1)} %add_add_fusion.2), channel_id=1, source_target_pairs={{0,24},{2,26},{4,28},{6,30},{8,0},{10,2},{12,4},{14,6},{16,8},{18,... | collective-permute-start | bytes 196616 | tf_op jit(solution)/shard_map/ppermute | solution.py:562
  159.1 5.8 %collective-permute-start.11 = (f32[32,512]{1,0:T(8,128)S(1)}, f32[32,512]{1,0:T(8,128)S(1)}, u32[]{:S(2)}, u32[]{:S(2)}) collective-permute-start(f32[32,512]{1,0:T(8,128)S(1)} %add_add_fusion.1), channel_id=1, source_target_pairs={{0,64},{2,66},{4,68},{6,70},{8,72},{10,74},{12,76},{14,78},{16,80}... | collective-permute-start | bytes 196616 | tf_op jit(solution)/shard_map/ppermute | solution.py:562
  160.3 5.5 %collective-permute-start.10 = (f32[32,512]{1,0:T(8,128)S(1)}, f32[32,512]{1,0:T(8,128)S(1)}, u32[]{:S(2)}, u32[]{:S(2)}) collective-permute-start(f32[32,512]{1,0:T(8,128)S(1)} %add_add_fusion.1), channel_id=1, source_target_pairs={{0,32},{2,34},{4,36},{6,38},{8,40},{10,42},{12,44},{14,46},{16,48}... | collective-permute-start | bytes 196616 | tf_op jit(solution)/shard_map/ppermute | solution.py:562
  161.1 4.7 %collective-permute-start.9 = (f32[32,512]{1,0:T(8,128)S(1)}, f32[32,512]{1,0:T(8,128)S(1)}, u32[]{:S(2)}, u32[]{:S(2)}) collective-permute-start(f32[32,512]{1,0:T(8,128)S(1)} %add_add_fusion.1), channel_id=1, source_target_pairs={{0,96},{2,98},{4,100},{6,102},{8,104},{10,106},{12,108},{14,110},{... | collective-permute-start | bytes 196616 | tf_op jit(solution)/shard_map/ppermute | solution.py:562
  165.8 1.3 collective-permute-start.12
  167.1 7.9 %copy-start.6 = (f32[32]{0:T(128)S(1)}, f32[32]{0:T(128)}, u32[]{:S(2)}) copy-start(f32[32]{0:T(128)} %param.15) | copy-start | bytes 388
  173.6 1.5 collective-permute-start.13
